TPU v7x, 256 devices: a whole 4x4x8 slice. The times are simulated.
256 devices in a mesh: ctx: 16 (over y, z_hi, core), ch: 16 (over z_lo, x).
Axes of the slice: x: 4, y: 4, z: 8 (z_hi: 2, z_lo: 4; z = z_hi * 4 + z_lo), core: 2. Of those that a mesh axis runs over, the one named last changes fastest.
Arguments:
- query: bfloat16 [16384, 2048], P('ctx', 'ch'), may hold values from -6 to 6
- key_in: bfloat16 [16384, 2048], P('ctx', 'ch'), may hold values from -6 to 6
- value: bfloat16 [16384, 2048], P('ctx', 'ch'), may hold values from -6 to 6
- short_taps: float32 [3, 3, 2048], P(None, None, 'ch'), may hold values from -3 to 3
- filt: float32 [16384, 2048], P('ctx', 'ch'), may hold values from -2 to 2
- skip_gain: float32 [2048], P('ch'), may hold values from -4 to 4
- out_weight: bfloat16 [2048, 2048], P('ch'), may hold values from -0.1875 to 0.1875
Outputs:
- mixed: bfloat16 [16384, 2048], P('ctx', 'ch')
All inputs are finite; a program needn't handle non-finite values.
Results may differ from a plain program's by a relative error of at most 0.0049.
Values may be sent and summed in bfloat16 or wider, within the bound.
A program may use at most 64 MiB of HBM per device.

v0:
```python
import math

import jax
import jax.numpy as jnp
from jax import lax
from jax.sharding import PartitionSpec as P

full_turn = 2.0 * math.pi
highest = lax.Precision.HIGHEST


def shifted(value, axis, steps):
    count = lax.axis_size(axis)
    initial, last = (max(0, -steps), min(count, count - steps))
    return lax.ppermute(value, axis, [(source, source + steps) for source in range(initial, last)])


def circle(counts, modulus):
    angle = full_turn * (counts % modulus).astype(jnp.float32) / modulus
    return (jnp.cos(angle), jnp.sin(angle))


def per_device(query, key_in, value, short_taps, filt, skip_gain, out_weight):
    ctx_count = lax.axis_size("ctx")
    ctx_pos = lax.axis_index("ctx")
    tok_rows, chan_dev = query.shape
    block_len = tok_rows // ctx_count
    fft_total = 2 * ctx_count * tok_rows
    coarse_count = 2 * ctx_count
    stacked = jnp.concatenate([query, key_in, value], axis=1)
    earlier = shifted(stacked[tok_rows - 2 :], "ctx", 1)
    extended = jnp.concatenate([earlier, stacked], axis=0).astype(jnp.float32)
    tap_rows = short_taps.reshape(3, 3 * chan_dev)
    smoothed = (
        tap_rows[0] * extended[2:] + tap_rows[1] * extended[1:-1] + tap_rows[2] * extended[:-2]
    )
    gate_part = smoothed[:, :chan_dev]
    key_part = smoothed[:, chan_dev : 2 * chan_dev]
    value_part = smoothed[:, 2 * chan_dev :]
    product = key_part * value_part
    coarse_freq = jnp.arange(coarse_count, dtype=jnp.int32)
    coarse_pos = jnp.arange(ctx_count, dtype=jnp.int32)
    fine_index = jnp.arange(tok_rows, dtype=jnp.int32)
    dense_cos, dense_sin = circle(fine_index[:, None] * fine_index[None, :], tok_rows)
    section_cos, section_sin = circle(coarse_freq[:, None] * coarse_pos[None, :], coarse_count)
    last_cos, last_sin = circle(coarse_pos[:, None] * coarse_freq[None, :], coarse_count)
    signal = jnp.concatenate([product, filt], axis=1)
    columns = lax.all_to_all(signal, "ctx", split_axis=0, concat_axis=0, tiled=True).reshape(
        ctx_count, block_len, 2 * chan_dev
    )
    sum_re = jnp.einsum("fp,pbc->fbc", section_cos, columns, precision=highest)
    sum_im = -jnp.einsum("fp,pbc->fbc", section_sin, columns, precision=highest)
    local_time = ctx_pos * block_len + jnp.arange(block_len, dtype=jnp.int32)
    twid_cos, twid_sin = circle(coarse_freq[:, None] * local_time[None, :], fft_total)
    twid_cos = twid_cos[:, :, None]
    twid_sin = twid_sin[:, :, None]
    z_re = twid_cos * sum_re + twid_sin * sum_im
    z_im = twid_cos * sum_im - twid_sin * sum_re
    spread = jnp.concatenate([z_re, z_im], axis=2).reshape(ctx_count, 2, block_len, 4 * chan_dev)
    items = lax.all_to_all(spread, "ctx", split_axis=0, concat_axis=2, tiled=True)
    fwd_cos = jnp.einsum("ft,...ta->...fa", dense_cos, items, precision=highest)
    fwd_sin = jnp.einsum("ft,...ta->...fa", dense_sin, items, precision=highest)
    real_part = fwd_cos[..., : 2 * chan_dev] + fwd_sin[..., 2 * chan_dev :]
    imag_part = fwd_cos[..., 2 * chan_dev :] - fwd_sin[..., : 2 * chan_dev]
    sig_re = real_part[..., :chan_dev]
    resp_re = real_part[..., chan_dev:]
    sig_im = imag_part[..., :chan_dev]
    resp_im = imag_part[..., chan_dev:]
    prod_re = sig_re * resp_re - sig_im * resp_im
    prod_im = sig_re * resp_im + sig_im * resp_re
    spectrum = jnp.concatenate([prod_re, prod_im], axis=-1)
    back_cos = jnp.einsum("tf,...fa->...ta", dense_cos, spectrum, precision=highest)
    back_sin = jnp.einsum("tf,...fa->...ta", dense_sin, spectrum, precision=highest)
    out_re = back_cos[..., :chan_dev] - back_sin[..., chan_dev:]
    out_im = back_cos[..., chan_dev:] + back_sin[..., :chan_dev]
    filtered = jnp.concatenate([out_re, out_im], axis=-1)[0]
    local_freq = ctx_pos * 2 + jnp.arange(2, dtype=jnp.int32)
    inv_cos, inv_sin = circle(local_freq[:, None] * fine_index[None, :], fft_total)
    inv_cos = inv_cos[:, :, None]
    inv_sin = inv_sin[:, :, None]
    part_re = filtered[..., :chan_dev]
    part_im = filtered[..., chan_dev:]
    turned_re = inv_cos * part_re - inv_sin * part_im
    turned_im = inv_cos * part_im + inv_sin * part_re
    turned = jnp.concatenate([turned_re, turned_im], axis=2)
    returned = lax.all_to_all(turned, "ctx", split_axis=1, concat_axis=0, tiled=True)
    merged = jnp.einsum("pf,fbc->pbc", last_cos, returned[..., :chan_dev], precision=highest)
    merged = merged - jnp.einsum(
        "pf,fbc->pbc", last_sin, returned[..., chan_dev:], precision=highest
    )
    merged = merged / fft_total
    conv = lax.all_to_all(merged, "ctx", split_axis=0, concat_axis=1, tiled=True).reshape(
        tok_rows, chan_dev
    )
    hidden = (gate_part * (conv + skip_gain * product)).astype(jnp.bfloat16)
    summed = lax.psum_scatter(
        lax.dot_general(
            out_weight, hidden, (((0,), (1,)), ((), ())), preferred_element_type=jnp.float32
        ),
        "ch",
        scatter_dimension=0,
        tiled=True,
    )
    return summed.astype(jnp.bfloat16).T


def solution(mesh):
    return jax.shard_map(
        per_device,
        mesh=mesh,
        in_specs=(
            P("ctx", "ch"),
            P("ctx", "ch"),
            P("ctx", "ch"),
            P(None, None, "ch"),
            P("ctx", "ch"),
            P("ch"),
            P("ch", None),
        ),
        out_specs=P("ctx", "ch"),
        check_vma=False,
    )
```

profile of v0, /device:TPU:8, one launch (start us, length us, event | category | flops | bytes accessed | tf_op | source)
XLA Modules:
  0.0 522.5 jit_solution(514718470694487922)
XLA Ops:
  6.5 0.0 copy-start
  6.5 1.1 constant_dynamic-update-slice_fusion.2
  7.6 1.0 constant_dynamic-update-slice_fusion.1
  8.6 1.0 constant_dynamic-update-slice_fusion
  9.6 1.9 collective-permute-start
  11.6 0.7 slice_bitcast_fusion.2
  12.3 7.1 %collective-permute-done = bf16[2,384]{1,0:T(2,128)(2,1)S(1)} collective-permute-done((bf16[2,384]{1,0:T(2,128)(2,1)S(1)}, bf16[2,384]{1,0:T(2,128)(2,1)S(1)}, u32[]{:S(2)}, u32[]{:S(2)}) %collective-permute-start) | collective-permute-done | bytes 1568 | tf_op jit(solution)/shard_map/ppermute | solution.py:15
  19.3 0.2 maximum_convert_fusion
  19.5 0.0 copy-start.1
  19.5 0.5 fusion.32
  20.0 0.1 slice_multiply_fusion.3
  20.1 0.5 copy-done.1
  20.6 1.1 pad_maximum_fusion.2
  21.7 10.7 %all-to-all-start = ((f32[16,64,256]{2,1,0:T(8,128)}), f32[16,64,256]{2,1,0:T(8,128)S(1)}, u32[]{:S(2)}, u32[]{:S(2)}) async-start(f32[16,64,256]{2,1,0:T(8,128)} %bitcast.92), calls=%async_computation | async-start | bytes 2097152 | tf_op jit(solution)/shard_map/all_to_all | solution.py:48
  32.3 0.2 fusion.50
  32.5 27.4 %all-to-all-done = f32[16,64,256]{2,1,0:T(8,128)S(1)} async-done(((f32[16,64,256]{2,1,0:T(8,128)}), f32[16,64,256]{2,1,0:T(8,128)S(1)}, u32[]{:S(2)}, u32[]{:S(2)}) %all-to-all-start) | async-done | bytes 1048608 | tf_op jit(solution)/shard_map/all_to_all | solution.py:48
  60.0 2.2 fusion.38
  62.2 2.8 multiply_add_fusion
  65.0 0.5 pad_maximum_fusion
  65.5 4.4 copy.29
  70.0 4.5 all-to-all-start.1
  74.4 0.3 reduce-scatter.2.cloned.1.call-start
  74.7 0.2 fusion.77
  74.9 51.6 %all-to-all-done.1 = f32[16,2,64,512]{3,2,1,0:T(8,128)} async-done(((f32[16,2,64,512]{3,2,1,0:T(8,128)}), f32[16,2,64,512]{3,2,1,0:T(8,128)}, u32[]{:S(2)}, u32[]{:S(2)}) %all-to-all-start.1) | async-done | bytes 4194336 | tf_op jit(solution)/shard_map/all_to_all | solution.py:60
  126.5 2.8 copy.20
  129.3 42.4 %fusion.14 = f32[1,2,1024,512]{2,3,1,0:T(8,128)S(1)} fusion(f32[2,1024,512]{2,1,0:T(8,128)S(1)} %bitcast.90), kind=kOutput, calls=%fused_computation.19 | convolution fusion | flops 12899581952 | bytes 8388608 | tf_op jit(solution)/shard_map/ft,...ta->...fa/dot_general | solution.py:61
  171.7 42.9 %fusion.17 = f32[1,2,1024,512]{2,3,1,0:T(8,128)S(1)} fusion(f32[2,1024,512]{2,1,0:T(8,128)S(1)} %bitcast.91), kind=kOutput, calls=%fused_computation.20 | convolution fusion | flops 12899581952 | bytes 8388608 | tf_op jit(solution)/shard_map/ft,...ta->...fa/dot_general | solution.py:62
  214.5 1.4 slice_add_fusion
  215.9 0.4 multiply_subtract_fusion.2
  216.4 22.9 %fusion.26 = f32[1,2,1024,256]{2,3,1,0:T(8,128)S(1)} fusion(f32[1,2,1024,128]{2,3,1,0:T(8,128)S(1)} %get-tuple-element.12, f32[1,2,1024,128]{2,3,1,0:T(8,128)S(1)} %get-tuple-element.11), kind=kOutput, calls=%fused_computation.30 | convolution fusion | flops 6457655296 | bytes 4194304 | tf_op jit(solution)/shard_map/tf,...fa->...ta/dot_general | solution.py:72
  239.2 23.3 %fusion.29 = f32[1,2,1024,256]{2,3,1,0:T(8,128)S(1)} fusion(f32[1,2,1024,128]{2,3,1,0:T(8,128)S(1)} %get-tuple-element.12, f32[1,2,1024,128]{2,3,1,0:T(8,128)S(1)} %get-tuple-element.11), kind=kOutput, calls=%fused_computation.31 | convolution fusion | flops 6457655296 | bytes 4194304 | tf_op jit(solution)/shard_map/tf,...fa->...ta/dot_general | solution.py:73
  262.5 0.6 slice_subtract_fusion.1
  263.1 0.2 maximum_bitcast_fusion.1
  263.3 0.4 multiply_subtract_fusion.1
  263.8 1.5 pad_maximum_fusion.1
  265.2 4.2 copy.23
  269.4 100.1 %all_to_all.51 = f32[2,1024,256]{2,0,1:T(2,128)S(1)} all-to-all(f32[2,1024,256]{2,0,1:T(2,128)} %copy.23), channel_id=1, replica_groups=mesh['ctx'=16,'ch'=16] {'ctx'}, dimensions={1} | all-to-all | bytes 4194304 | tf_op jit(solution)/shard_map/all_to_all | solution.py:86
  369.5 0.2 copy.24
  369.7 2.9 copy.25
  372.6 0.0 copy-start.2
  372.6 3.7 all_to_all.45
  376.3 1.9 fusion.36
  378.2 1.9 fusion.34
  380.1 0.2 copy.26
  380.3 20.9 %all_to_all.52 = f32[16,64,128]{2,1,0:T(8,128)S(1)} all-to-all(f32[16,64,128]{2,1,0:T(8,128)S(1)} %copy.26), channel_id=1, replica_groups=mesh['ctx'=16,'ch'=16] {'ctx'}, dimensions={0} | all-to-all | bytes 1048576 | tf_op jit(solution)/shard_map/all_to_all | solution.py:92
  401.2 0.0 copy-done.2
  401.2 0.1 fusion.42
  401.3 0.0 copy-done
  401.3 4.5 convolution_bitcast_fusion
  405.8 0.0 reduce-scatter.2.cloned.1.call-update
  405.8 107.6 %reduce-scatter.2.cloned.1.call-done = f32[128,1024]{0,1:T(8,128)} async-done(((f32[2048,1024]{0,1:T(8,128)}), f32[128,1024]{0,1:T(8,128)}) %reduce-scatter.2.cloned.1.call-update) | async-done | bytes 524304 | tf_op jit(solution)/shard_map/reduce_scatter | solution.py:96
  513.4 1.8 convert_bitcast_fusion
  (3 shorter events, 0.0 us)
Async XLA Ops:
  6.5 394.8 %copy-start = (bf16[128,2048]{1,0:T(8,128)(2,1)S(1)}, bf16[128,2048]{1,0:T(8,128)(2,1)}, u32[]{:S(2)}) copy-start(bf16[128,2048]{1,0:T(8,128)(2,1)} %param.13) | copy-start | bytes 1572868
  9.6 9.7 %collective-permute-start = (bf16[2,384]{1,0:T(2,128)(2,1)S(1)}, bf16[2,384]{1,0:T(2,128)(2,1)S(1)}, u32[]{:S(2)}, u32[]{:S(2)}) collective-permute-start(bf16[2,384]{1,0:T(2,128)(2,1)S(1)} %slice.107), channel_id=1, source_target_pairs={{0,16},{16,32},{32,48},{48,64},{64,80},{80,96},{96,112},{112,128},... | collective-permute-start | bytes 4616 | tf_op jit(solution)/shard_map/ppermute | solution.py:15
  19.5 1.0 copy-start.1
  21.7 38.3 %all-to-all-start = ((f32[16,64,256]{2,1,0:T(8,128)}), f32[16,64,256]{2,1,0:T(8,128)S(1)}, u32[]{:S(2)}, u32[]{:S(2)}) async-start(f32[16,64,256]{2,1,0:T(8,128)} %bitcast.92), calls=%async_computation | async-start | bytes 2097152 | tf_op jit(solution)/shard_map/all_to_all | solution.py:48
  70.0 56.6 %all-to-all-start.1 = ((f32[16,2,64,512]{3,2,1,0:T(8,128)}), f32[16,2,64,512]{3,2,1,0:T(8,128)}, u32[]{:S(2)}, u32[]{:S(2)}) async-start(f32[16,2,64,512]{3,2,1,0:T(8,128)} %bitcast.88), calls=%async_computation.1 | async-start | bytes 8388608 | tf_op jit(solution)/shard_map/all_to_all | solution.py:60
  74.4 439.0 %reduce-scatter.2.cloned.1.call-start = ((), (), s32[]{:S(2)}) async-start(), calls=%async_computation.5 | async-start | bytes 8912896 | tf_op jit(solution)/shard_map/reduce_scatter | solution.py:96
  372.6 28.6 %copy-start.2 = (f32[128]{0:T(128)S(1)}, f32[128]{0:T(128)}, u32[]{:S(2)}) copy-start(f32[128]{0:T(128)} %param.12) | copy-start | bytes 1540
Sparse Core Ops, SparseCore 0:
  406.0 107.4 reduce-scatter.1
where the time goes:
time: 530 us; the launch traced here: 522 us
  waiting for transfers between devices  194 us (37%)
  matrix products  145 us (27%)
  blocking collectives  121 us (23%)
  local copies, waits for them, and re-layouts  22.6 us (4%)
  starting transfers between devices  17.3 us (3%)
  between operations  14.1 us (3%)
  other arithmetic  9.1 us (2%)
    reduce_scatter x1, waiting for transfers between devices, per_device(): lax.psum_scatter(lax.dot_general(out_weight, hidden, (((0,), (1,)), ((),...  108 us
    all_to_all x1, blocking collectives, per_device(): lax.all_to_all(turned, 'ctx', split_axis=1, concat_axis=0, tiled=True)  100 us
    all_to_all x1, waiting for transfers between devices, per_device(): lax.all_to_all(spread, 'ctx', split_axis=0, concat_axis=2, tiled=True)  51.6 us
    dot_general x1, matrix products, per_device(): fwd_sin = jnp.einsum('ft,...ta->...fa', dense_sin, items, precision=highest)  42.9 us
    dot_general x1, matrix products, per_device(): fwd_cos = jnp.einsum('ft,...ta->...fa', dense_cos, items, precision=highest)  42.4 us
    all_to_all x1, waiting for transfers between devices, per_device(): lax.all_to_all(signal, 'ctx', split_axis=0, concat_axis=0, tiled=True)  27.4 us
    dot_general x1, matrix products, per_device(): jnp.einsum('tf,...fa->...ta', dense_sin, spectrum, precision=highest)  23.3 us
    dot_general x1, matrix products, per_device(): jnp.einsum('tf,...fa->...ta', dense_cos, spectrum, precision=highest)  22.9 us
  transfers between devices with their start and end apart: 4, of which 4 were waited for; matrix products, arithmetic and copies ran while one was open for 0% of the time, Pallas kernels for 0%

commit v1 on v0

v1 whole, which is shorter than its diff:
```python
import functools

import jax
import jax.numpy as jnp
import ml_dtypes
import numpy as np
from jax import lax
from jax.experimental import pallas as pl
from jax.experimental.pallas import tpu as pltpu
from jax.sharding import PartitionSpec as P

CTX = 16
CH = 16
ROWS = 1024
LANES = 128
TILES = ROWS // 128
OWN = LANES // CTX
HALF = 1024
PIECE = TILES * OWN
F32 = jnp.float32
BF16 = jnp.bfloat16
MESH = pl.DeviceIdType.MESH


def hi_lo(matrix):
    high = matrix.astype(ml_dtypes.bfloat16)
    low = (matrix - high.astype(np.float64)).astype(ml_dtypes.bfloat16)
    return high, low


def transform_matrices():
    index = np.arange(128, dtype=np.float64)
    shifted = index + 0.25
    turn = 2.0 * np.pi
    first = turn * np.outer(shifted, index) / 128.0
    forward = np.concatenate([np.cos(first), -np.sin(first)], axis=0)
    first_hi, first_lo = hi_lo(forward)
    first_cat = np.concatenate([first_hi, first_lo], axis=1)
    twiddle = turn * np.outer(shifted, index) / 16384.0
    twiddles = np.stack([np.cos(twiddle), -np.sin(twiddle)]).astype(np.float32)
    second = turn * np.outer(index, index) / 128.0
    cos, sin = np.cos(second), np.sin(second)
    ahead = np.block([[cos, -sin], [sin, cos]])
    back = np.block([[cos, sin], [-sin, cos]])
    last = np.concatenate([np.cos(first).T, -np.sin(first).T], axis=1) / 16384.0
    squares = np.stack([first_cat, *hi_lo(ahead), *hi_lo(back)])
    finals = np.stack(hi_lo(last))
    return squares, finals, twiddles


def split(value):
    high = value.astype(BF16)
    return high, (value - high.astype(F32)).astype(BF16)


def mul(a, b):
    return jnp.dot(a, b, preferred_element_type=F32)


def spectrum_pair(load, squares, tw_re, tw_im):
    points = jnp.concatenate([load(0), load(1)], axis=1).astype(BF16)
    stage = mul(squares[0], jnp.concatenate([points, points], axis=0))
    parts = []
    for which in range(2):
        re = stage[:128, 128 * which : 128 * which + 128]
        im = stage[128:, 128 * which : 128 * which + 128]
        parts.append(jnp.concatenate([re * tw_re - im * tw_im, re * tw_im + im * tw_re], axis=1))
    high, low = split(jnp.concatenate(parts, axis=0))
    return mul(high, squares[1]) + mul(low, squares[1]) + mul(high, squares[2])


def inverse_pair(signal, response, squares, finals, tw_re, tw_im):
    s_re, s_im = signal[:, :128], signal[:, 128:]
    r_re, r_im = response[:, :128], response[:, 128:]
    high, low = split(
        jnp.concatenate([s_re * r_re - s_im * r_im, s_re * r_im + s_im * r_re], axis=1)
    )
    stage = mul(high, squares[3]) + mul(low, squares[3]) + mul(high, squares[4])
    turned = []
    for which in range(2):
        re = stage[128 * which : 128 * which + 128, :128]
        im = stage[128 * which : 128 * which + 128, 128:]
        turned.append(jnp.concatenate([re * tw_re + im * tw_im, im * tw_re - re * tw_im], axis=0))
    high, low = split(jnp.concatenate(turned, axis=1))
    both = mul(finals[0], high) + mul(finals[0], low) + mul(finals[1], high)
    return both[:, :128], both[:, 128:]


def kernel(
    q_hbm, k_hbm, v_hbm, taps_hbm, filt_hbm, skip_hbm, w_hbm, sq_hbm, fin_hbm, tw_hbm,
    out_hbm,
    q_in, k_in, v_in, taps, filt, skip, squares, finals, twiddle,
    ext, halo_out, halo_in, gate, product, stage, pieces, f_out, p_out, y_out, f_in, p_in, y_in,
    points, response, turned, hidden, hidden_in, weights, mixed,
    load_sem, halo_sem, send_sem, recv_sem, w_send, w_recv, core_send, core_recv,
    h_send, h_recv, o_send, o_recv,
):
    c, h = lax.axis_index("ctx"), lax.axis_index("ch")
    core = lax.rem(c, 2)
    sibling = c + 1 - 2 * core
    zb, at = h // 8, lax.rem(h, 8)
    za, x = at // 4, lax.rem(h, 4)
    across = (1 - zb) * 8 + at
    beside = zb * 8 + (1 - za) * 4 + x
    diagonal = (1 - zb) * 8 + (1 - za) * 4 + x

    loads = [
        pltpu.make_async_copy(src, dst, load_sem.at[i])
        for i, (src, dst) in enumerate(
            [
                (filt_hbm, filt), (k_hbm, k_in), (v_hbm, v_in), (q_hbm, q_in), (taps_hbm, taps),
                (skip_hbm, skip), (sq_hbm, squares), (fin_hbm, finals), (tw_hbm, twiddle),
                (w_hbm.at[pl.ds(0, 64), pl.ds(pl.multiple_of(zb * HALF, HALF), HALF)], weights.at[h, 0]),
                (w_hbm.at[pl.ds(64, 64), pl.ds(pl.multiple_of(zb * HALF, HALF), HALF)], weights.at[h, 1]),
            ]
        )
    ]
    for load in loads:
        load.start()

    barrier = pltpu.get_barrier_semaphore()

    @pl.loop(1, 16)
    def _(step):
        pl.semaphore_signal(
            barrier, inc=1, device_id={"ctx": lax.rem(c + step, CTX)}, device_id_type=MESH
        )
        pl.semaphore_signal(
            barrier, inc=1, device_id={"ch": lax.rem(h + step, CH)}, device_id_type=MESH
        )

    def to_pieces(tile, value):
        stage[:, OWN * tile : OWN * tile + OWN, :] = value.T.reshape(CTX, OWN, 128)

    def exchange(kind, source, target, step):
        peer = lax.rem(c + step, CTX)
        return pltpu.make_async_remote_copy(
            src_ref=source.at[peer], dst_ref=target.at[c], send_sem=send_sem.at[kind, peer],
            recv_sem=recv_sem.at[kind, c], device_id={"ctx": peer}, device_id_type=MESH,
        )

    def arrival(kind, source, target, step):
        peer = lax.rem(c + step, CTX)
        return pltpu.make_async_remote_copy(
            src_ref=source.at[peer], dst_ref=target.at[peer], send_sem=send_sem.at[kind, peer],
            recv_sem=recv_sem.at[kind, peer], device_id={"ctx": peer}, device_id_type=MESH,
        )

    def start_exchange(kind, source, target):
        @pl.loop(1, CTX)
        def _(step):
            exchange(kind, source, target, step).start()

        target[c] = source[c]

    def wait_exchange(kind, source, target):
        @pl.loop(1, CTX)
        def _(step):
            arrival(kind, source, target, step).wait_recv()

    def weight_copy(block, peer):
        return pltpu.make_async_remote_copy(
            src_ref=weights.at[block, core], dst_ref=weights.at[block, core],
            send_sem=w_send.at[block, peer], recv_sem=w_recv.at[block],
            device_id={"ch": peer}, device_id_type=MESH,
        )

    def weight_out():
        return pltpu.make_async_remote_copy(
            src_ref=w_hbm.at[
                pl.ds(pl.multiple_of(core * 64, 64), 64),
                pl.ds(pl.multiple_of((1 - zb) * HALF, HALF), HALF),
            ],
            dst_ref=weights.at[h, core],
            send_sem=w_send.at[h, across], recv_sem=w_recv.at[h],
            device_id={"ch": across}, device_id_type=MESH,
        )

    def along_x(block, step):
        return weight_copy(block, (h // 4) * 4 + lax.rem(x + step, 4))

    def send_along_x(block):
        @pl.loop(1, 4)
        def _(step):
            along_x(block, step).start()

    def core_copy(block):
        return pltpu.make_async_remote_copy(
            src_ref=weights.at[block, core], dst_ref=weights.at[block, core],
            send_sem=core_send.at[block], recv_sem=core_recv.at[block],
            device_id={"ctx": sibling}, device_id_type=MESH,
        )

    def core_arrival(block):
        return pltpu.make_async_remote_copy(
            src_ref=weights.at[block, 1 - core], dst_ref=weights.at[block, 1 - core],
            send_sem=core_send.at[block], recv_sem=core_recv.at[block],
            device_id={"ctx": sibling}, device_id_type=MESH,
        )

    loads[0].wait()
    for tile in range(TILES):
        to_pieces(tile, filt[128 * tile : 128 * tile + 128, :])
    f_out[...] = stage[...].astype(BF16)

    for load in loads[1:]:
        load.wait()
    for i, source in enumerate((k_in, v_in, q_in)):
        halo_out[16 * i : 16 * i + 16, :] = source[ROWS - 16 :, :]

    pl.semaphore_wait(barrier, 30)

    halo = pltpu.make_async_remote_copy(
        src_ref=halo_out, dst_ref=halo_in, send_sem=halo_sem.at[0], recv_sem=halo_sem.at[1],
        device_id={"ctx": lax.rem(c + 1, CTX)}, device_id_type=MESH,
    )
    halo.start()
    start_exchange(0, f_out, f_in)
    weight_out().start()
    weight_copy(h, beside).start()
    send_along_x(h)

    for i, source in enumerate((k_in, v_in, q_in)):
        ext[i, 8:, :] = source[...].astype(F32)

    def smooth(tile):
        first = 128 * tile + 8
        sums = []
        for i, which in enumerate((1, 2, 0)):
            total = taps[0, which : which + 1, :] * ext[i, first : first + 128, :]
            total += taps[1, which : which + 1, :] * ext[i, first - 1 : first + 127, :]
            total += taps[2, which : which + 1, :] * ext[i, first - 2 : first + 126, :]
            sums.append(total)
        both = sums[0] * sums[1]
        gate[tile] = sums[2]
        product[tile] = both
        to_pieces(tile, both)

    for tile in range(1, TILES):
        smooth(tile)
    halo.wait()
    for i in range(3):
        before = halo_in[16 * i : 16 * i + 16, :].astype(F32)[8:]
        ext[i, :8, :] = jnp.where(c == 0, jnp.zeros_like(before), before)
    smooth(0)
    p_out[...] = stage[...].astype(BF16)
    start_exchange(1, p_out, p_in)

    tw_re, tw_im = twiddle[0], twiddle[1]

    weight_copy(across, across).wait_recv()
    weight_copy(across, beside).start()
    send_along_x(across)
    weight_copy(beside, beside).wait_recv()
    send_along_x(beside)

    def gathered(source):
        points[...] = source[...].astype(F32).reshape(CTX * PIECE, 128)

    def loader(pair):
        return lambda which: points[pl.ds(2 * pair + which, 128, stride=OWN), :]

    wait_exchange(0, f_out, f_in)
    gathered(f_in)

    @pl.loop(0, OWN // 2)
    def _(pair):
        response[pair] = spectrum_pair(loader(pair), squares, tw_re, tw_im)

    weight_copy(diagonal, beside).wait_recv()
    send_along_x(diagonal)

    wait_exchange(1, p_out, p_in)
    gathered(p_in)

    @pl.loop(0, OWN // 2)
    def _(pair):
        signal = spectrum_pair(loader(pair), squares, tw_re, tw_im)
        low, high = inverse_pair(signal, response[pair], squares, finals, tw_re, tw_im)
        rows = pl.ds(pl.multiple_of(16 * pair, 16), 16)
        y_out[:, rows, :] = jnp.concatenate(
            [low.reshape(CTX, TILES, 128), high.reshape(CTX, TILES, 128)], axis=1
        ).astype(BF16)

    start_exchange(2, y_out, y_in)

    @pl.loop(1, 4)
    def _(step):
        peer_x = lax.rem(x + step, 4)

        @pl.loop(0, 4)
        def _(z):
            weight_copy(4 * z + peer_x, h).wait_recv()

    @pl.loop(1, CH)
    def _(step):
        core_copy(lax.rem(h + step, CH)).start()

    wait_exchange(2, y_out, y_in)
    turned[...] = y_in[...].astype(F32).reshape(CTX * PIECE, 128)

    def hidden_copy(half, tile):
        peer = 8 * half + tile
        return pltpu.make_async_remote_copy(
            src_ref=hidden.at[tile], dst_ref=hidden_in.at[h], send_sem=h_send.at[peer],
            recv_sem=h_recv.at[h], device_id={"ch": peer}, device_id_type=MESH,
        )

    @pl.loop(0, TILES)
    def _(step):
        tile = lax.rem(at + step, TILES)
        conv = turned[pl.ds(tile, 128, stride=TILES), :].T
        value = (gate[tile] * (conv + skip[...] * product[tile])).astype(BF16)
        hidden[tile] = value
        hidden_copy(1 - zb, tile).start()

        @pl.when(step == 0)
        def _():
            hidden_in[h] = value

        @pl.when(step > 0)
        def _():
            hidden_copy(zb, tile).start()

    @pl.loop(1, CH)
    def _(step):
        core_arrival(lax.rem(h + step, CH)).wait_recv()

    @pl.loop(1, CH)
    def _(step):
        peer = lax.rem(h + step, CH)
        pltpu.make_async_remote_copy(
            src_ref=hidden_in.at[peer], dst_ref=hidden_in.at[peer], send_sem=h_send.at[peer],
            recv_sem=h_recv.at[peer], device_id={"ch": peer}, device_id_type=MESH,
        ).wait_recv()

    lhs = jnp.concatenate([hidden_in[i] for i in range(CH)], axis=1)

    def mixed_copy(tile):
        return pltpu.make_async_remote_copy(
            src_ref=mixed.at[tile], dst_ref=out_hbm.at[pl.ds(pl.multiple_of(128 * at, 128), 128), :],
            send_sem=o_send.at[tile], recv_sem=o_recv.at[at],
            device_id={"ch": 8 * zb + tile}, device_id_type=MESH,
        )

    own_copy = pltpu.make_async_copy(
        mixed.at[at], out_hbm.at[pl.ds(pl.multiple_of(128 * at, 128), 128), :], load_sem.at[0]
    )

    for part in range(4):
        rhs = weights[:, :, :, 256 * part : 256 * part + 256].reshape(CH * LANES, 256)
        value = mul(lhs, rhs).astype(BF16)
        for i in range(2):
            tile = 2 * part + i
            mixed[tile] = value[:, 128 * i : 128 * i + 128]

            @pl.when(at != tile)
            def _():
                mixed_copy(tile).start()

            @pl.when(at == tile)
            def _():
                own_copy.start()

    @pl.loop(1, CTX)
    def _(step):
        arrival(0, f_out, f_in, step).wait_send()
        arrival(1, p_out, p_in, step).wait_send()
        arrival(2, y_out, y_in, step).wait_send()

    weight_out().wait_send()
    weight_copy(h, beside).wait_send()
    weight_copy(across, beside).wait_send()

    @pl.loop(1, 4)
    def _(step):
        along_x(h, step).wait_send()
        along_x(across, step).wait_send()
        along_x(beside, step).wait_send()
        along_x(diagonal, step).wait_send()

    @pl.loop(1, CH)
    def _(step):
        core_copy(lax.rem(h + step, CH)).wait_send()

    @pl.loop(0, TILES)
    def _(step):
        tile = lax.rem(at + step, TILES)
        hidden_copy(1 - zb, tile).wait_send()

        @pl.when(step > 0)
        def _():
            hidden_copy(zb, tile).wait_send()
            mixed_copy(tile).wait_send()
            pltpu.make_async_remote_copy(
                src_ref=mixed.at[tile],
                dst_ref=out_hbm.at[pl.ds(pl.multiple_of(128 * tile, 128), 128), :],
                send_sem=o_send.at[tile], recv_sem=o_recv.at[tile],
                device_id={"ch": 8 * zb + tile}, device_id_type=MESH,
            ).wait_recv()

    own_copy.wait()


def per_device(query, key_in, value, short_taps, filt, skip_gain, out_weight):
    squares, finals, twiddles = transform_matrices()
    any_space = pl.BlockSpec(memory_space=pl.ANY)
    dma = pltpu.SemaphoreType.DMA
    piece = (CTX, PIECE, 128)
    return pl.pallas_call(
        kernel,
        out_shape=jax.ShapeDtypeStruct((ROWS, LANES), BF16),
        in_specs=[any_space] * 10,
        out_specs=any_space,
        scratch_shapes=[
            pltpu.VMEM((ROWS, LANES), BF16),
            pltpu.VMEM((ROWS, LANES), BF16),
            pltpu.VMEM((ROWS, LANES), BF16),
            pltpu.VMEM((3, 3, LANES), F32),
            pltpu.VMEM((ROWS, LANES), F32),
            pltpu.VMEM((1, LANES), F32),
            pltpu.VMEM(squares.shape, BF16),
            pltpu.VMEM(finals.shape, BF16),
            pltpu.VMEM(twiddles.shape, F32),
            pltpu.VMEM((3, ROWS + 8, LANES), F32),
            pltpu.VMEM((48, LANES), BF16),
            pltpu.VMEM((48, LANES), BF16),
            pltpu.VMEM((TILES, 128, LANES), F32),
            pltpu.VMEM((TILES, 128, LANES), F32),
            pltpu.VMEM(piece, F32),
            pltpu.VMEM((8, 128), F32),
            pltpu.VMEM(piece, BF16),
            pltpu.VMEM(piece, BF16),
            pltpu.VMEM(piece, BF16),
            pltpu.VMEM(piece, BF16),
            pltpu.VMEM(piece, BF16),
            pltpu.VMEM(piece, BF16),
            pltpu.VMEM((CTX * PIECE, 128), F32),
            pltpu.VMEM((OWN // 2, 256, 256), F32),
            pltpu.VMEM((CTX * PIECE, 128), F32),
            pltpu.VMEM((TILES, 128, LANES), BF16),
            pltpu.VMEM((CH, 128, LANES), BF16),
            pltpu.VMEM((CH, 2, 64, HALF), BF16),
            pltpu.VMEM((TILES, 128, LANES), BF16),
            dma((11,)),
            dma((2,)),
            dma((3, CTX)),
            dma((3, CTX)),
            dma((CH, CH)),
            dma((CH,)),
            dma((CH,)),
            dma((CH,)),
            dma((CH,)),
            dma((CH,)),
            dma((TILES,)),
            dma((TILES,)),
        ],
        compiler_params=pltpu.CompilerParams(
            collective_id=0, has_side_effects=True, vmem_limit_bytes=40 * 1024 * 1024
        ),
        cost_estimate=pl.CostEstimate(flops=3_000_000_000, bytes_accessed=4_000_000, transcendentals=0),
    )(
        query, key_in, value, short_taps, filt, skip_gain.reshape(1, LANES), out_weight,
        jnp.asarray(squares), jnp.asarray(finals), jnp.asarray(twiddles),
    )


def solution(mesh):
    return jax.shard_map(
        per_device,
        mesh=mesh,
        in_specs=(
            P("ctx", "ch"),
            P("ctx", "ch"),
            P("ctx", "ch"),
            P(None, None, "ch"),
            P("ctx", "ch"),
            P("ch"),
            P("ch", None),
        ),
        out_specs=P("ctx", "ch"),
        check_vma=False,
    )
```

time: 530 us -> 80.6 us (0.15)
  the two profiles are of different devices: /device:TPU:8 before, /device:TPU:1 now
where the time goes in v1:
time: 80.6 us; the launch traced here: 79.7 us
  Pallas kernels  69.8 us (87%)
  local copies, waits for them, and re-layouts  9.88 us (12%)
    pallas_call x1, Pallas kernels, per_device(): pl.pallas_call(kernel, out_shape=jax.ShapeDtypeStruct((ROWS, LANES), BF16...  69.8 us
    unnamed x21, local copies, waits for them, and re-layouts  9.88 us

profile of v1, /device:TPU:1, one launch (start us, length us, event | category | flops | bytes accessed | tf_op | source)
XLA Modules:
  0.0 79.7 jit_solution(3374252556168620111)
XLA Ops:
  0.0 0.0 copy-start.6
  0.0 0.7 copy-done.6
  0.7 0.0 copy-start
  0.7 1.0 %copy-done = f32[1024,128]{1,0:T(8,128)S(1)} copy-done((f32[1024,128]{1,0:T(8,128)S(1)}, f32[1024,128]{1,0:T(8,128)}, u32[]{:S(2)}) %copy-start) | copy-done | bytes 524312
  1.7 0.0 copy-start.1
  1.7 1.0 %copy-done.1 = bf16[128,2048]{1,0:T(8,128)(2,1)S(1)} copy-done((bf16[128,2048]{1,0:T(8,128)(2,1)S(1)}, bf16[128,2048]{1,0:T(8,128)(2,1)}, u32[]{:S(2)}) %copy-start.1) | copy-done | bytes 524312
  2.7 0.0 copy-start.2
  2.7 0.9 %copy-done.2 = bf16[1024,128]{1,0:T(8,128)(2,1)S(1)} copy-done((bf16[1024,128]{1,0:T(8,128)(2,1)S(1)}, bf16[1024,128]{1,0:T(8,128)(2,1)}, u32[]{:S(2)}) %copy-start.2) | copy-done | bytes 262168
  3.7 0.0 copy-start.3
  3.7 0.9 %copy-done.3 = bf16[1024,128]{1,0:T(8,128)(2,1)S(1)} copy-done((bf16[1024,128]{1,0:T(8,128)(2,1)S(1)}, bf16[1024,128]{1,0:T(8,128)(2,1)}, u32[]{:S(2)}) %copy-start.3) | copy-done | bytes 262168
  4.6 0.0 copy-start.4
  4.6 0.9 %copy-done.4 = bf16[1024,128]{1,0:T(8,128)(2,1)S(1)} copy-done((bf16[1024,128]{1,0:T(8,128)(2,1)S(1)}, bf16[1024,128]{1,0:T(8,128)(2,1)}, u32[]{:S(2)}) %copy-start.4) | copy-done | bytes 262168
  5.6 0.0 copy-start.5
  5.6 0.7 copy-done.5
  6.3 0.0 copy-start.7
  6.3 1.1 %copy-done.7 = bf16[5,256,256]{2,1,0:T(8,128)(2,1)S(1)} copy-done((bf16[5,256,256]{2,1,0:T(8,128)(2,1)S(1)}, bf16[5,256,256]{2,1,0:T(8,128)(2,1)}, u32[]{:S(2)}) %copy-start.7) | copy-done | bytes 655384
  7.4 0.0 copy-start.8
  7.4 0.9 %copy-done.8 = f32[2,128,128]{2,1,0:T(8,128)S(1)} copy-done((f32[2,128,128]{2,1,0:T(8,128)S(1)}, f32[2,128,128]{2,1,0:T(8,128)}, u32[]{:S(2)}) %copy-start.8) | copy-done | bytes 131096
  8.3 0.0 copy-start.9
  8.3 0.9 %copy-done.9 = bf16[2,128,256]{2,1,0:T(8,128)(2,1)S(1)} copy-done((bf16[2,128,256]{2,1,0:T(8,128)(2,1)S(1)}, bf16[2,128,256]{2,1,0:T(8,128)(2,1)}, u32[]{:S(2)}) %copy-start.9) | copy-done | bytes 131096
  9.2 69.8 %shard_map.100 = bf16[1024,128]{1,0:T(8,128)(2,1)S(1)} custom-call(bf16[1024,128]{1,0:T(8,128)(2,1)S(1)} %copy-done.2, bf16[1024,128]{1,0:T(8,128)(2,1)S(1)} %copy-done.3, bf16[1024,128]{1,0:T(8,128)(2,1)S(1)} %copy-done.4, f32[3,3,128]{2,1,0:T(4,128)S(1)} %copy-done.5, f32[1024,128]{1,0:T(8,128)S(1)} %copy-done, f32[1,128]{1,0:T(1,128)S(1)} %bitcast.1, ...), custom_call_target="tpu_custom_call" | custom-call | flops 3000000000 | bytes 4000000 | tf_op jit(solution)/shard_map/pallas_call | solution.py:410
  79.0 0.7 copy.12
Async XLA Ops:
  0.0 0.7 copy-start.6
  0.7 1.0 %copy-start = (f32[1024,128]{1,0:T(8,128)S(1)}, f32[1024,128]{1,0:T(8,128)}, u32[]{:S(2)}) copy-start(f32[1024,128]{1,0:T(8,128)} %filt_hbm.1) | copy-start | bytes 1572868
  1.7 1.0 %copy-start.1 = (bf16[128,2048]{1,0:T(8,128)(2,1)S(1)}, bf16[128,2048]{1,0:T(8,128)(2,1)}, u32[]{:S(2)}) copy-start(bf16[128,2048]{1,0:T(8,128)(2,1)} %w_hbm.1) | copy-start | bytes 1572868
  2.7 0.9 %copy-start.2 = (bf16[1024,128]{1,0:T(8,128)(2,1)S(1)}, bf16[1024,128]{1,0:T(8,128)(2,1)}, u32[]{:S(2)}) copy-start(bf16[1024,128]{1,0:T(8,128)(2,1)} %q_hbm.1) | copy-start | bytes 786436
  3.7 0.9 %copy-start.3 = (bf16[1024,128]{1,0:T(8,128)(2,1)S(1)}, bf16[1024,128]{1,0:T(8,128)(2,1)}, u32[]{:S(2)}) copy-start(bf16[1024,128]{1,0:T(8,128)(2,1)} %k_hbm.1) | copy-start | bytes 786436
  4.6 0.9 %copy-start.4 = (bf16[1024,128]{1,0:T(8,128)(2,1)S(1)}, bf16[1024,128]{1,0:T(8,128)(2,1)}, u32[]{:S(2)}) copy-start(bf16[1024,128]{1,0:T(8,128)(2,1)} %v_hbm.1) | copy-start | bytes 786436
  5.6 0.7 copy-start.5
  6.3 1.1 %copy-start.7 = (bf16[5,256,256]{2,1,0:T(8,128)(2,1)S(1)}, bf16[5,256,256]{2,1,0:T(8,128)(2,1)}, u32[]{:S(2)}) copy-start(bf16[5,256,256]{2,1,0:T(8,128)(2,1)} %constant.6.clone.sq_hbm) | copy-start | bytes 1966084
  7.4 0.9 %copy-start.8 = (f32[2,128,128]{2,1,0:T(8,128)S(1)}, f32[2,128,128]{2,1,0:T(8,128)}, u32[]{:S(2)}) copy-start(f32[2,128,128]{2,1,0:T(8,128)} %constant.8.clone.tw_hbm) | copy-start | bytes 393220
  8.3 0.9 %copy-start.9 = (bf16[2,128,256]{2,1,0:T(8,128)(2,1)S(1)}, bf16[2,128,256]{2,1,0:T(8,128)(2,1)}, u32[]{:S(2)}) copy-start(bf16[2,128,256]{2,1,0:T(8,128)(2,1)} %constant.7.clone.fin_hbm) | copy-start | bytes 393220

commit v2 on v1

--- a/solution.py
+++ b/solution.py
@@ -16,7 +16,10 @@
 TILES = ROWS // 128
 OWN = LANES // CTX
 HALF = 1024
-PIECE = TILES * OWN
+GROUPS = 2
+PART = LANES // GROUPS
+MINE = OWN // GROUPS
+PIECE = MINE * TILES
 F32 = jnp.float32
 BF16 = jnp.bfloat16
 MESH = pl.DeviceIdType.MESH
@@ -90,8 +93,9 @@
     q_hbm, k_hbm, v_hbm, taps_hbm, filt_hbm, skip_hbm, w_hbm, sq_hbm, fin_hbm, tw_hbm,
     out_hbm,
     q_in, k_in, v_in, taps, filt, skip, squares, finals, twiddle,
-    ext, halo_out, halo_in, gate, product, stage, pieces, f_out, p_out, y_out, f_in, p_in, y_in,
-    points, response, turned, hidden, hidden_in, weights, mixed,
+    ext, halo_out, halo_in, filt_t, gate_t, product_t, skipped_t,
+    f_out, p_out, y_out, f_in, p_in, y_in,
+    response, rows_t, hidden, hidden_in, weights, lhs, total, mixed,
     load_sem, halo_sem, send_sem, recv_sem, w_send, w_recv, core_send, core_recv,
     h_send, h_recv, o_send, o_recv,
 ):
@@ -129,34 +133,41 @@
             barrier, inc=1, device_id={"ch": lax.rem(h + step, CH)}, device_id_type=MESH
         )
 
-    def to_pieces(tile, value):
-        stage[:, OWN * tile : OWN * tile + OWN, :] = value.T.reshape(CTX, OWN, 128)
-
-    def exchange(kind, source, target, step):
+    def turn(target, tile, value):
+        target[pl.ds(tile, LANES, stride=TILES), :] = value.T
+
+    def pack(target, source):
+        for g in range(GROUPS):
+            rows = source[PART * TILES * g : PART * TILES * (g + 1), :]
+            target[g] = rows.reshape(CTX, PIECE, 128).astype(BF16)
+
+    def exchange(kind, g, source, target, step):
         peer = lax.rem(c + step, CTX)
         return pltpu.make_async_remote_copy(
-            src_ref=source.at[peer], dst_ref=target.at[c], send_sem=send_sem.at[kind, peer],
-            recv_sem=recv_sem.at[kind, c], device_id={"ctx": peer}, device_id_type=MESH,
-        )
-
-    def arrival(kind, source, target, step):
+            src_ref=source.at[g, peer], dst_ref=target.at[g, c],
+            send_sem=send_sem.at[kind, g, peer], recv_sem=recv_sem.at[kind, g, c],
+            device_id={"ctx": peer}, device_id_type=MESH,
+        )
+
+    def arrival(kind, g, source, target, step):
         peer = lax.rem(c + step, CTX)
         return pltpu.make_async_remote_copy(
-            src_ref=source.at[peer], dst_ref=target.at[peer], send_sem=send_sem.at[kind, peer],
-            recv_sem=recv_sem.at[kind, peer], device_id={"ctx": peer}, device_id_type=MESH,
-        )
-
-    def start_exchange(kind, source, target):
+            src_ref=source.at[g, peer], dst_ref=target.at[g, peer],
+            send_sem=send_sem.at[kind, g, peer], recv_sem=recv_sem.at[kind, g, peer],
+            device_id={"ctx": peer}, device_id_type=MESH,
+        )
+
+    def start_exchange(kind, g, source, target):
         @pl.loop(1, CTX)
         def _(step):
-            exchange(kind, source, target, step).start()
-
-        target[c] = source[c]
-
-    def wait_exchange(kind, source, target):
+            exchange(kind, g, source, target, step).start()
+
+        target[g, c] = source[g, c]
+
+    def wait_exchange(kind, g, source, target):
         @pl.loop(1, CTX)
         def _(step):
-            arrival(kind, source, target, step).wait_recv()
+            arrival(kind, g, source, target, step).wait_recv()
 
     def weight_copy(block, peer):
         return pltpu.make_async_remote_copy(
@@ -200,13 +211,30 @@
 
     loads[0].wait()
     for tile in range(TILES):
-        to_pieces(tile, filt[128 * tile : 128 * tile + 128, :])
-    f_out[...] = stage[...].astype(BF16)
+        turn(filt_t, tile, filt[128 * tile : 128 * tile + 128, :])
+    pack(f_out, filt_t)
 
     for load in loads[1:]:
         load.wait()
     for i, source in enumerate((k_in, v_in, q_in)):
         halo_out[16 * i : 16 * i + 16, :] = source[ROWS - 16 :, :]
+        ext[i, 8:, :] = source[...].astype(F32)
+
+    def smooth(tile):
+        first = 128 * tile + 8
+        sums = []
+        for i, which in enumerate((1, 2, 0)):
+            part = taps[0, which : which + 1, :] * ext[i, first : first + 128, :]
+            part += taps[1, which : which + 1, :] * ext[i, first - 1 : first + 127, :]
+            part += taps[2, which : which + 1, :] * ext[i, first - 2 : first + 126, :]
+            sums.append(part)
+        both = sums[0] * sums[1]
+        turn(product_t, tile, both)
+        turn(skipped_t, tile, skip[...] * both)
+        turn(gate_t, tile, sums[2])
+
+    for tile in range(1, TILES):
+        smooth(tile)
 
     pl.semaphore_wait(barrier, 30)
 
@@ -215,38 +243,20 @@
         device_id={"ctx": lax.rem(c + 1, CTX)}, device_id_type=MESH,
     )
     halo.start()
-    start_exchange(0, f_out, f_in)
+    for g in range(GROUPS):
+        start_exchange(0, g, f_out, f_in)
     weight_out().start()
     weight_copy(h, beside).start()
     send_along_x(h)
 
-    for i, source in enumerate((k_in, v_in, q_in)):
-        ext[i, 8:, :] = source[...].astype(F32)
-
-    def smooth(tile):
-        first = 128 * tile + 8
-        sums = []
-        for i, which in enumerate((1, 2, 0)):
-            total = taps[0, which : which + 1, :] * ext[i, first : first + 128, :]
-            total += taps[1, which : which + 1, :] * ext[i, first - 1 : first + 127, :]
-            total += taps[2, which : which + 1, :] * ext[i, first - 2 : first + 126, :]
-            sums.append(total)
-        both = sums[0] * sums[1]
-        gate[tile] = sums[2]
-        product[tile] = both
-        to_pieces(tile, both)
-
-    for tile in range(1, TILES):
-        smooth(tile)
     halo.wait()
     for i in range(3):
         before = halo_in[16 * i : 16 * i + 16, :].astype(F32)[8:]
         ext[i, :8, :] = jnp.where(c == 0, jnp.zeros_like(before), before)
     smooth(0)
-    p_out[...] = stage[...].astype(BF16)
-    start_exchange(1, p_out, p_in)
-
-    tw_re, tw_im = twiddle[0], twiddle[1]
+    pack(p_out, product_t)
+    for g in range(GROUPS):
+        start_exchange(1, g, p_out, p_in)
 
     weight_copy(across, across).wait_recv()
     weight_copy(across, beside).start()
@@ -254,35 +264,60 @@
     weight_copy(beside, beside).wait_recv()
     send_along_x(beside)
 
-    def gathered(source):
-        points[...] = source[...].astype(F32).reshape(CTX * PIECE, 128)
-
-    def loader(pair):
-        return lambda which: points[pl.ds(2 * pair + which, 128, stride=OWN), :]
-
-    wait_exchange(0, f_out, f_in)
-    gathered(f_in)
-
-    @pl.loop(0, OWN // 2)
-    def _(pair):
-        response[pair] = spectrum_pair(loader(pair), squares, tw_re, tw_im)
+    tw_re, tw_im = twiddle[0], twiddle[1]
+
+    def loader(source, g, pair):
+        both = source[g, :, 16 * pair : 16 * pair + 16, :].astype(F32)
+        return lambda which: both[:, 8 * which : 8 * which + 8, :].reshape(128, 128)
+
+    for g in range(GROUPS):
+        wait_exchange(0, g, f_out, f_in)
+        for pair in range(MINE // 2):
+            response[g, pair] = spectrum_pair(loader(f_in, g, pair), squares, tw_re, tw_im)
 
     weight_copy(diagonal, beside).wait_recv()
     send_along_x(diagonal)
 
-    wait_exchange(1, p_out, p_in)
-    gathered(p_in)
-
-    @pl.loop(0, OWN // 2)
-    def _(pair):
-        signal = spectrum_pair(loader(pair), squares, tw_re, tw_im)
-        low, high = inverse_pair(signal, response[pair], squares, finals, tw_re, tw_im)
-        rows = pl.ds(pl.multiple_of(16 * pair, 16), 16)
-        y_out[:, rows, :] = jnp.concatenate(
-            [low.reshape(CTX, TILES, 128), high.reshape(CTX, TILES, 128)], axis=1
-        ).astype(BF16)
-
-    start_exchange(2, y_out, y_in)
+    for g in range(GROUPS):
+        wait_exchange(1, g, p_out, p_in)
+        for pair in range(MINE // 2):
+            signal = spectrum_pair(loader(p_in, g, pair), squares, tw_re, tw_im)
+            low, high = inverse_pair(signal, response[g, pair], squares, finals, tw_re, tw_im)
+            y_out[g, :, 16 * pair : 16 * pair + 16, :] = jnp.concatenate(
+                [low.reshape(CTX, TILES, 128), high.reshape(CTX, TILES, 128)], axis=1
+            ).astype(BF16)
+        start_exchange(2, g, y_out, y_in)
+
+    def hidden_copy(g, half, tile):
+        peer = 8 * half + tile
+        return pltpu.make_async_remote_copy(
+            src_ref=hidden.at[g, tile], dst_ref=hidden_in.at[g, h],
+            send_sem=h_send.at[g, peer], recv_sem=h_recv.at[g, h],
+            device_id={"ch": peer}, device_id_type=MESH,
+        )
+
+    for g in range(GROUPS):
+        wait_exchange(2, g, y_out, y_in)
+        for quarter in range(4):
+            rows = slice(PART * TILES // 4 * quarter, PART * TILES // 4 * (quarter + 1))
+            whole = slice(PART * TILES * g + rows.start, PART * TILES * g + rows.stop)
+            conv = y_in[g, 4 * quarter : 4 * quarter + 4].astype(F32).reshape(4 * PIECE, 128)
+            rows_t[rows, :] = gate_t[whole, :] * (conv + skipped_t[whole, :])
+
+        @pl.loop(0, TILES)
+        def _(step):
+            tile = lax.rem(at + step, TILES)
+            value = rows_t[pl.ds(tile, PART, stride=TILES), :].astype(BF16)
+            hidden[g, tile] = value
+            hidden_copy(g, 1 - zb, tile).start()
+
+            @pl.when(step == 0)
+            def _():
+                hidden_in[g, h] = value
+
+            @pl.when(step > 0)
+            def _():
+                hidden_copy(g, zb, tile).start()
 
     @pl.loop(1, 4)
     def _(step):
@@ -296,45 +331,9 @@
     def _(step):
         core_copy(lax.rem(h + step, CH)).start()
 
-    wait_exchange(2, y_out, y_in)
-    turned[...] = y_in[...].astype(F32).reshape(CTX * PIECE, 128)
-
-    def hidden_copy(half, tile):
-        peer = 8 * half + tile
-        return pltpu.make_async_remote_copy(
-            src_ref=hidden.at[tile], dst_ref=hidden_in.at[h], send_sem=h_send.at[peer],
-            recv_sem=h_recv.at[h], device_id={"ch": peer}, device_id_type=MESH,
-        )
-
-    @pl.loop(0, TILES)
-    def _(step):
-        tile = lax.rem(at + step, TILES)
-        conv = turned[pl.ds(tile, 128, stride=TILES), :].T
-        value = (gate[tile] * (conv + skip[...] * product[tile])).astype(BF16)
-        hidden[tile] = value
-        hidden_copy(1 - zb, tile).start()
-
-        @pl.when(step == 0)
-        def _():
-            hidden_in[h] = value
-
-        @pl.when(step > 0)
-        def _():
-            hidden_copy(zb, tile).start()
-
     @pl.loop(1, CH)
     def _(step):
         core_arrival(lax.rem(h + step, CH)).wait_recv()
-
-    @pl.loop(1, CH)
-    def _(step):
-        peer = lax.rem(h + step, CH)
-        pltpu.make_async_remote_copy(
-            src_ref=hidden_in.at[peer], dst_ref=hidden_in.at[peer], send_sem=h_send.at[peer],
-            recv_sem=h_recv.at[peer], device_id={"ch": peer}, device_id_type=MESH,
-        ).wait_recv()
-
-    lhs = jnp.concatenate([hidden_in[i] for i in range(CH)], axis=1)
 
     def mixed_copy(tile):
         return pltpu.make_async_remote_copy(
@@ -347,26 +346,47 @@
         mixed.at[at], out_hbm.at[pl.ds(pl.multiple_of(128 * at, 128), 128), :], load_sem.at[0]
     )
 
-    for part in range(4):
-        rhs = weights[:, :, :, 256 * part : 256 * part + 256].reshape(CH * LANES, 256)
-        value = mul(lhs, rhs).astype(BF16)
-        for i in range(2):
-            tile = 2 * part + i
-            mixed[tile] = value[:, 128 * i : 128 * i + 128]
-
-            @pl.when(at != tile)
-            def _():
-                mixed_copy(tile).start()
-
-            @pl.when(at == tile)
-            def _():
-                own_copy.start()
-
-    @pl.loop(1, CTX)
-    def _(step):
-        arrival(0, f_out, f_in, step).wait_send()
-        arrival(1, p_out, p_in, step).wait_send()
-        arrival(2, y_out, y_in, step).wait_send()
+    for g in range(GROUPS):
+
+        @pl.loop(1, CH)
+        def _(step):
+            peer = lax.rem(h + step, CH)
+            pltpu.make_async_remote_copy(
+                src_ref=hidden_in.at[g, peer], dst_ref=hidden_in.at[g, peer],
+                send_sem=h_send.at[g, peer], recv_sem=h_recv.at[g, peer],
+                device_id={"ch": peer}, device_id_type=MESH,
+            ).wait_recv()
+
+        for i in range(CH // 2):
+            two = hidden_in[g, 2 * i : 2 * i + 2].astype(F32).reshape(128, 128)
+            lhs[:, 128 * i : 128 * i + 128] = two.T.astype(BF16)
+
+        for part in range(4):
+            cut = slice(256 * part, 256 * part + 256)
+            value = mul(lhs[...], weights[:, g, :, cut].reshape(CH * PART, 256))
+            if g < GROUPS - 1:
+                total[:, cut] = value
+                continue
+            value = (total[:, cut] + value).astype(BF16)
+            for i in range(2):
+                tile = 2 * part + i
+                mixed[tile] = value[:, 128 * i : 128 * i + 128]
+
+                @pl.when(at != tile)
+                def _():
+                    mixed_copy(tile).start()
+
+                @pl.when(at == tile)
+                def _():
+                    own_copy.start()
+
+    for g in range(GROUPS):
+
+        @pl.loop(1, CTX)
+        def _(step):
+            arrival(0, g, f_out, f_in, step).wait_send()
+            arrival(1, g, p_out, p_in, step).wait_send()
+            arrival(2, g, y_out, y_in, step).wait_send()
 
     weight_out().wait_send()
     weight_copy(h, beside).wait_send()
@@ -386,11 +406,13 @@
     @pl.loop(0, TILES)
     def _(step):
         tile = lax.rem(at + step, TILES)
-        hidden_copy(1 - zb, tile).wait_send()
+        for g in range(GROUPS):
+            hidden_copy(g, 1 - zb, tile).wait_send()
 
         @pl.when(step > 0)
         def _():
-            hidden_copy(zb, tile).wait_send()
+            for g in range(GROUPS):
+                hidden_copy(g, zb, tile).wait_send()
             mixed_copy(tile).wait_send()
             pltpu.make_async_remote_copy(
                 src_ref=mixed.at[tile],
@@ -404,14 +426,14 @@
 
 def per_device(query, key_in, value, short_taps, filt, skip_gain, out_weight):
     squares, finals, twiddles = transform_matrices()
-    any_space = pl.BlockSpec(memory_space=pl.ANY)
+    in_hbm = pl.BlockSpec(memory_space=pltpu.HBM)
     dma = pltpu.SemaphoreType.DMA
-    piece = (CTX, PIECE, 128)
+    piece = (GROUPS, CTX, PIECE, 128)
     return pl.pallas_call(
         kernel,
         out_shape=jax.ShapeDtypeStruct((ROWS, LANES), BF16),
-        in_specs=[any_space] * 10,
-        out_specs=any_space,
+        in_specs=[in_hbm] * 10,
+        out_specs=in_hbm,
         scratch_shapes=[
             pltpu.VMEM((ROWS, LANES), BF16),
             pltpu.VMEM((ROWS, LANES), BF16),
@@ -425,38 +447,39 @@
             pltpu.VMEM((3, ROWS + 8, LANES), F32),
             pltpu.VMEM((48, LANES), BF16),
             pltpu.VMEM((48, LANES), BF16),
-            pltpu.VMEM((TILES, 128, LANES), F32),
-            pltpu.VMEM((TILES, 128, LANES), F32),
-            pltpu.VMEM(piece, F32),
-            pltpu.VMEM((8, 128), F32),
+            pltpu.VMEM((ROWS, 128), F32),
+            pltpu.VMEM((ROWS, 128), F32),
+            pltpu.VMEM((ROWS, 128), F32),
+            pltpu.VMEM((ROWS, 128), F32),
             pltpu.VMEM(piece, BF16),
             pltpu.VMEM(piece, BF16),
             pltpu.VMEM(piece, BF16),
             pltpu.VMEM(piece, BF16),
             pltpu.VMEM(piece, BF16),
             pltpu.VMEM(piece, BF16),
-            pltpu.VMEM((CTX * PIECE, 128), F32),
-            pltpu.VMEM((OWN // 2, 256, 256), F32),
-            pltpu.VMEM((CTX * PIECE, 128), F32),
-            pltpu.VMEM((TILES, 128, LANES), BF16),
-            pltpu.VMEM((CH, 128, LANES), BF16),
+            pltpu.VMEM((GROUPS, MINE // 2, 256, 256), F32),
+            pltpu.VMEM((PART * TILES, 128), F32),
+            pltpu.VMEM((GROUPS, TILES, PART, 128), BF16),
+            pltpu.VMEM((GROUPS, CH, PART, 128), BF16),
             pltpu.VMEM((CH, 2, 64, HALF), BF16),
+            pltpu.VMEM((128, CH * PART), BF16),
+            pltpu.VMEM((128, HALF), F32),
             pltpu.VMEM((TILES, 128, LANES), BF16),
             dma((11,)),
             dma((2,)),
-            dma((3, CTX)),
-            dma((3, CTX)),
+            dma((3, GROUPS, CTX)),
+            dma((3, GROUPS, CTX)),
             dma((CH, CH)),
             dma((CH,)),
             dma((CH,)),
             dma((CH,)),
-            dma((CH,)),
-            dma((CH,)),
+            dma((GROUPS, CH)),
+            dma((GROUPS, CH)),
             dma((TILES,)),
             dma((TILES,)),
         ],
         compiler_params=pltpu.CompilerParams(
-            collective_id=0, has_side_effects=True, vmem_limit_bytes=40 * 1024 * 1024
+            collective_id=0, has_side_effects=True, vmem_limit_bytes=60 * 1024 * 1024
         ),
         cost_estimate=pl.CostEstimate(flops=3_000_000_000, bytes_accessed=4_000_000, transcendentals=0),
     )(

time: 80.6 us -> 66.5 us (0.83)
  local copies, waits for them, and re-layouts: 9.88 us -> 1.67 us
  Pallas kernels: 69.8 us -> 64.2 us
    unnamed x21 -> x1, local copies, waits for them, and re-layouts: 9.88 us -> 1.67 us
    pallas_call x1, Pallas kernels: 69.8 us -> 64.2 us  [per_device(): pl.pallas_call(kernel, out_shape=jax.ShapeDtypeStruct((ROWS, LANES), BF16...]
where the time goes in v2:
time: 66.5 us; the launch traced here: 65.9 us
  Pallas kernels  64.2 us (97%)
  local copies, waits for them, and re-layouts  1.67 us (3%)
    pallas_call x1, Pallas kernels, per_device(): pl.pallas_call(kernel, out_shape=jax.ShapeDtypeStruct((ROWS, LANES), BF16...  64.2 us
    unnamed x1, local copies, waits for them, and re-layouts  1.67 us

profile of v2, /device:TPU:1, one launch (start us, length us, event | category | flops | bytes accessed | tf_op | source)
XLA Modules:
  0.0 65.9 jit_solution(4316700549888434265)
XLA Ops:
  0.0 64.2 %shard_map.100 = bf16[1024,128]{1,0:T(8,128)(2,1)} custom-call(bf16[1024,128]{1,0:T(8,128)(2,1)} %q_hbm.1, bf16[1024,128]{1,0:T(8,128)(2,1)} %k_hbm.1, bf16[1024,128]{1,0:T(8,128)(2,1)} %v_hbm.1, f32[3,3,128]{2,1,0:T(4,128)} %taps_hbm.1, f32[1024,128]{1,0:T(8,128)} %filt_hbm.1, f32[1,128]{1,0:T(1,128)} %bitcast.1, bf16[128,2048]{1,0:T(8,128)(2,1)} %w_hbm.1, ...), custom_call_target="tpu_custom_call" | custom-call | flops 3000000000 | bytes 4000000 | tf_op jit(solution)/shard_map/pallas_call | solution.py:432
  64.2 1.7 %copy.12 = bf16[1024,128]{1,0:T(8,128)(2,1)} copy(bf16[1024,128]{1,0:T(8,128)(2,1)} %shard_map.100) | data formatting | bytes 524288

commit v3 on v2

--- a/solution.py
+++ b/solution.py
@@ -96,12 +96,13 @@
     ext, halo_out, halo_in, filt_t, gate_t, product_t, skipped_t,
     f_out, p_out, y_out, f_in, p_in, y_in,
     response, rows_t, hidden, hidden_in, weights, lhs, total, mixed,
-    load_sem, halo_sem, send_sem, recv_sem, w_send, w_recv, core_send, core_recv,
+    load_sem, halo_sem, send_sem, recv_sem, z_send, w_send, w_recv, x_recv, core_send, core_recv,
     h_send, h_recv, o_send, o_recv,
 ):
     c, h = lax.axis_index("ctx"), lax.axis_index("ch")
     core = lax.rem(c, 2)
     sibling = c + 1 - 2 * core
+    y = c // 4
     zb, at = h // 8, lax.rem(h, 8)
     za, x = at // 4, lax.rem(h, 4)
     across = (1 - zb) * 8 + at
@@ -169,31 +170,142 @@
         def _(step):
             arrival(kind, g, source, target, step).wait_recv()
 
-    def weight_copy(block, peer):
-        return pltpu.make_async_remote_copy(
+    column = (h, across, beside, diagonal)
+
+    def quarter(block, q):
+        return weights.at[block, core, pl.ds(pl.multiple_of(16 * q, 16), 16)]
+
+    def along_z(i):
+        half = zb if i == 1 else 1 - zb
+        return pltpu.make_async_remote_copy(
+            src_ref=w_hbm.at[
+                pl.ds(pl.multiple_of(core * 64 + y * 16, 16), 16),
+                pl.ds(pl.multiple_of(half * HALF, HALF), HALF),
+            ],
+            dst_ref=quarter(h, y), send_sem=z_send.at[i], recv_sem=w_recv.at[h, y],
+            device_id={"ch": column[i + 1]}, device_id_type=MESH,
+        )
+
+    def along_y(block, step):
+        peer = lax.rem(y + step, 4)
+        return pltpu.make_async_remote_copy(
+            src_ref=quarter(block, y), dst_ref=quarter(block, y),
+            send_sem=w_send.at[block, peer, 0], recv_sem=w_recv.at[block, y],
+            device_id={"ctx": 4 * peer + lax.rem(c, 4)}, device_id_type=MESH,
+        )
+
+    def along_x(block, step, whole):
+        peer = lax.rem(x + step, 4)
+        part = weights.at[block, core] if whole else quarter(block, y)
+        return pltpu.make_async_remote_copy(
+            src_ref=part, dst_ref=part, send_sem=w_send.at[block, peer, 1],
+            recv_sem=x_recv.at[block] if whole else w_recv.at[block, y],
+            device_id={"ch": (h // 4) * 4 + peer}, device_id_type=MESH,
+        )
+
+    def wait_quarter(block, q):
+        pltpu.make_async_remote_copy(
+            src_ref=quarter(block, q), dst_ref=quarter(block, q),
+            send_sem=w_send.at[block, 0, 0], recv_sem=w_recv.at[block, q],
+            device_id={"ch": across}, device_id_type=MESH,
+        ).wait_recv()
+
+    def wait_whole(block):
+        pltpu.make_async_remote_copy(
             src_ref=weights.at[block, core], dst_ref=weights.at[block, core],
-            send_sem=w_send.at[block, peer], recv_sem=w_recv.at[block],
-            device_id={"ch": peer}, device_id_type=MESH,
-        )
-
-    def weight_out():
-        return pltpu.make_async_remote_copy(
-            src_ref=w_hbm.at[
-                pl.ds(pl.multiple_of(core * 64, 64), 64),
-                pl.ds(pl.multiple_of((1 - zb) * HALF, HALF), HALF),
-            ],
-            dst_ref=weights.at[h, core],
-            send_sem=w_send.at[h, across], recv_sem=w_recv.at[h],
+            send_sem=w_send.at[block, 0, 0], recv_sem=x_recv.at[block],
             device_id={"ch": across}, device_id_type=MESH,
-        )
-
-    def along_x(block, step):
-        return weight_copy(block, (h // 4) * 4 + lax.rem(x + step, 4))
-
-    def send_along_x(block):
+        ).wait_recv()
+
+    def on_core(which):
+        return pl.when(core == which)
+
+    def steps_of_four(body):
+        pl.loop(1, 4)(body)
+
+    def other_columns(body):
         @pl.loop(1, 4)
         def _(step):
-            along_x(block, step).start()
+            peer = lax.rem(x + step, 4)
+
+            @pl.loop(0, 4)
+            def _(z):
+                body(4 * z + peer)
+
+    def weights_start():
+        for i in range(3):
+            along_z(i).start()
+
+        @on_core(0)
+        def _():
+            steps_of_four(lambda step: along_x(h, step, True).start())
+
+        @on_core(1)
+        def _():
+            steps_of_four(lambda step: along_x(h, step, False).start())
+
+    def weights_second():
+        for block in column[1:]:
+            wait_quarter(block, y)
+
+            @on_core(0)
+            def _():
+                steps_of_four(lambda step: along_y(block, step).start())
+
+            @on_core(1)
+            def _():
+                steps_of_four(lambda step: along_x(block, step, False).start())
+
+    def weights_third():
+        @on_core(0)
+        def _():
+            for block in column[1:]:
+                steps_of_four(lambda step: wait_quarter(block, lax.rem(y + step, 4)))
+                steps_of_four(lambda step: along_x(block, step, True).start())
+
+        @on_core(1)
+        def _():
+            for block in column[1:]:
+                steps_of_four(lambda step: along_y(block, step).start())
+
+            def onward(block):
+                wait_quarter(block, y)
+                steps_of_four(lambda step: along_y(block, step).start())
+
+            other_columns(onward)
+
+    def weights_gathered():
+        @on_core(0)
+        def _():
+            other_columns(wait_whole)
+
+        @on_core(1)
+        def _():
+            @pl.loop(1, CH)
+            def _(step):
+                block = lax.rem(h + step, CH)
+                steps_of_four(lambda turn: wait_quarter(block, lax.rem(y + turn, 4)))
+
+    def weights_drain():
+        for i in range(3):
+            along_z(i).wait_send()
+
+        @on_core(0)
+        def _():
+            for block in column:
+                steps_of_four(lambda step: along_x(block, step, True).wait_send())
+            for block in column[1:]:
+                steps_of_four(lambda step: along_y(block, step).wait_send())
+
+        @on_core(1)
+        def _():
+            for block in column:
+                steps_of_four(lambda step: along_x(block, step, False).wait_send())
+
+            @pl.loop(1, CH)
+            def _(step):
+                block = lax.rem(h + step, CH)
+                steps_of_four(lambda turn: along_y(block, turn).wait_send())
 
     def core_copy(block):
         return pltpu.make_async_remote_copy(
@@ -245,9 +357,7 @@
     halo.start()
     for g in range(GROUPS):
         start_exchange(0, g, f_out, f_in)
-    weight_out().start()
-    weight_copy(h, beside).start()
-    send_along_x(h)
+    weights_start()
 
     halo.wait()
     for i in range(3):
@@ -258,11 +368,6 @@
     for g in range(GROUPS):
         start_exchange(1, g, p_out, p_in)
 
-    weight_copy(across, across).wait_recv()
-    weight_copy(across, beside).start()
-    send_along_x(across)
-    weight_copy(beside, beside).wait_recv()
-    send_along_x(beside)
 
     tw_re, tw_im = twiddle[0], twiddle[1]
 
@@ -275,9 +380,8 @@
         for pair in range(MINE // 2):
             response[g, pair] = spectrum_pair(loader(f_in, g, pair), squares, tw_re, tw_im)
 
-    weight_copy(diagonal, beside).wait_recv()
-    send_along_x(diagonal)
-
+
+    weights_second()
     for g in range(GROUPS):
         wait_exchange(1, g, p_out, p_in)
         for pair in range(MINE // 2):
@@ -288,6 +392,7 @@
             ).astype(BF16)
         start_exchange(2, g, y_out, y_in)
 
+    weights_third()
     def hidden_copy(g, half, tile):
         peer = 8 * half + tile
         return pltpu.make_async_remote_copy(
@@ -298,10 +403,10 @@
 
     for g in range(GROUPS):
         wait_exchange(2, g, y_out, y_in)
-        for quarter in range(4):
-            rows = slice(PART * TILES // 4 * quarter, PART * TILES // 4 * (quarter + 1))
+        for fourth in range(4):
+            rows = slice(PART * TILES // 4 * fourth, PART * TILES // 4 * (fourth + 1))
             whole = slice(PART * TILES * g + rows.start, PART * TILES * g + rows.stop)
-            conv = y_in[g, 4 * quarter : 4 * quarter + 4].astype(F32).reshape(4 * PIECE, 128)
+            conv = y_in[g, 4 * fourth : 4 * fourth + 4].astype(F32).reshape(4 * PIECE, 128)
             rows_t[rows, :] = gate_t[whole, :] * (conv + skipped_t[whole, :])
 
         @pl.loop(0, TILES)
@@ -319,13 +424,7 @@
             def _():
                 hidden_copy(g, zb, tile).start()
 
-    @pl.loop(1, 4)
-    def _(step):
-        peer_x = lax.rem(x + step, 4)
-
-        @pl.loop(0, 4)
-        def _(z):
-            weight_copy(4 * z + peer_x, h).wait_recv()
+    weights_gathered()
 
     @pl.loop(1, CH)
     def _(step):
@@ -388,16 +487,7 @@
             arrival(1, g, p_out, p_in, step).wait_send()
             arrival(2, g, y_out, y_in, step).wait_send()
 
-    weight_out().wait_send()
-    weight_copy(h, beside).wait_send()
-    weight_copy(across, beside).wait_send()
-
-    @pl.loop(1, 4)
-    def _(step):
-        along_x(h, step).wait_send()
-        along_x(across, step).wait_send()
-        along_x(beside, step).wait_send()
-        along_x(diagonal, step).wait_send()
+    weights_drain()
 
     @pl.loop(1, CH)
     def _(step):
@@ -469,7 +559,9 @@
             dma((2,)),
             dma((3, GROUPS, CTX)),
             dma((3, GROUPS, CTX)),
-            dma((CH, CH)),
+            dma((3,)),
+            dma((CH, 4, 2)),
+            dma((CH, 4)),
             dma((CH,)),
             dma((CH,)),
             dma((CH,)),

time: 66.5 us -> 63 us (0.947)
  Pallas kernels: 64.2 us -> 61.2 us
    pallas_call x1, Pallas kernels: 64.2 us -> 61.2 us  [per_device(): pl.pallas_call(kernel, out_shape=jax.ShapeDtypeStruct((ROWS, LANES), BF16...]
where the time goes in v3:
time: 63 us; the launch traced here: 62.9 us
  Pallas kernels  61.2 us (97%)
  local copies, waits for them, and re-layouts  1.67 us (3%)
    pallas_call x1, Pallas kernels, per_device(): pl.pallas_call(kernel, out_shape=jax.ShapeDtypeStruct((ROWS, LANES), BF16...  61.2 us
    unnamed x1, local copies, waits for them, and re-layouts  1.67 us

profile of v3, /device:TPU:1, one launch (start us, length us, event | category | flops | bytes accessed | tf_op | source)
XLA Modules:
  0.0 62.9 jit_solution(4974340589338000574)
XLA Ops:
  0.0 61.2 %shard_map.100 = bf16[1024,128]{1,0:T(8,128)(2,1)} custom-call(bf16[1024,128]{1,0:T(8,128)(2,1)} %q_hbm.1, bf16[1024,128]{1,0:T(8,128)(2,1)} %k_hbm.1, bf16[1024,128]{1,0:T(8,128)(2,1)} %v_hbm.1, f32[3,3,128]{2,1,0:T(4,128)} %taps_hbm.1, f32[1024,128]{1,0:T(8,128)} %filt_hbm.1, f32[1,128]{1,0:T(1,128)} %bitcast.1, bf16[128,2048]{1,0:T(8,128)(2,1)} %w_hbm.1, ...), custom_call_target="tpu_custom_call" | custom-call | flops 3000000000 | bytes 4000000 | tf_op jit(solution)/shard_map/pallas_call | solution.py:522
  61.2 1.7 %copy.12 = bf16[1024,128]{1,0:T(8,128)(2,1)} copy(bf16[1024,128]{1,0:T(8,128)(2,1)} %shard_map.100) | data formatting | bytes 524288

commit v4 on v3

--- a/solution.py
+++ b/solution.py
@@ -96,7 +96,7 @@
     ext, halo_out, halo_in, filt_t, gate_t, product_t, skipped_t,
     f_out, p_out, y_out, f_in, p_in, y_in,
     response, rows_t, hidden, hidden_in, weights, lhs, total, mixed,
-    load_sem, halo_sem, send_sem, recv_sem, z_send, w_send, w_recv, x_recv, core_send, core_recv,
+    load_sem, halo_sem, send_sem, recv_sem, w_send, w_recv, y_recv, x_recv, core_send, core_recv,
     h_send, h_recv, o_send, o_recv,
 ):
     c, h = lax.axis_index("ctx"), lax.axis_index("ch")
@@ -146,17 +146,18 @@
         peer = lax.rem(c + step, CTX)
         return pltpu.make_async_remote_copy(
             src_ref=source.at[g, peer], dst_ref=target.at[g, c],
-            send_sem=send_sem.at[kind, g, peer], recv_sem=recv_sem.at[kind, g, c],
+            send_sem=send_sem.at[kind, g], recv_sem=recv_sem.at[kind, g],
             device_id={"ctx": peer}, device_id_type=MESH,
         )
 
-    def arrival(kind, g, source, target, step):
-        peer = lax.rem(c + step, CTX)
-        return pltpu.make_async_remote_copy(
-            src_ref=source.at[g, peer], dst_ref=target.at[g, peer],
-            send_sem=send_sem.at[kind, g, peer], recv_sem=recv_sem.at[kind, g, peer],
-            device_id={"ctx": peer}, device_id_type=MESH,
-        )
+    def sum_of(part, send, recv):
+        return pltpu.make_async_remote_copy(
+            src_ref=part, dst_ref=part, send_sem=send, recv_sem=recv,
+            device_id={"ctx": sibling}, device_id_type=MESH,
+        )
+
+    def pieces(kind, g, target):
+        return sum_of(target.at[g, pl.ds(0, CTX - 1)], send_sem.at[kind, g], recv_sem.at[kind, g])
 
     def start_exchange(kind, g, source, target):
         @pl.loop(1, CTX)
@@ -165,10 +166,8 @@
 
         target[g, c] = source[g, c]
 
-    def wait_exchange(kind, g, source, target):
-        @pl.loop(1, CTX)
-        def _(step):
-            arrival(kind, g, source, target, step).wait_recv()
+    def wait_exchange(kind, g, target):
+        pieces(kind, g, target).wait_recv()
 
     column = (h, across, beside, diagonal)
 
@@ -182,15 +181,15 @@
                 pl.ds(pl.multiple_of(core * 64 + y * 16, 16), 16),
                 pl.ds(pl.multiple_of(half * HALF, HALF), HALF),
             ],
-            dst_ref=quarter(h, y), send_sem=z_send.at[i], recv_sem=w_recv.at[h, y],
+            dst_ref=quarter(h, y), send_sem=w_send.at[0], recv_sem=w_recv.at[h],
             device_id={"ch": column[i + 1]}, device_id_type=MESH,
         )
 
-    def along_y(block, step):
+    def along_y(block, step, low):
         peer = lax.rem(y + step, 4)
         return pltpu.make_async_remote_copy(
             src_ref=quarter(block, y), dst_ref=quarter(block, y),
-            send_sem=w_send.at[block, peer, 0], recv_sem=w_recv.at[block, y],
+            send_sem=w_send.at[0], recv_sem=y_recv.at[block] if low else y_recv.at[y],
             device_id={"ctx": 4 * peer + lax.rem(c, 4)}, device_id_type=MESH,
         )
 
@@ -198,24 +197,13 @@
         peer = lax.rem(x + step, 4)
         part = weights.at[block, core] if whole else quarter(block, y)
         return pltpu.make_async_remote_copy(
-            src_ref=part, dst_ref=part, send_sem=w_send.at[block, peer, 1],
-            recv_sem=x_recv.at[block] if whole else w_recv.at[block, y],
+            src_ref=part, dst_ref=part, send_sem=w_send.at[0],
+            recv_sem=x_recv.at[0] if whole else w_recv.at[block],
             device_id={"ch": (h // 4) * 4 + peer}, device_id_type=MESH,
         )
 
-    def wait_quarter(block, q):
-        pltpu.make_async_remote_copy(
-            src_ref=quarter(block, q), dst_ref=quarter(block, q),
-            send_sem=w_send.at[block, 0, 0], recv_sem=w_recv.at[block, q],
-            device_id={"ch": across}, device_id_type=MESH,
-        ).wait_recv()
-
-    def wait_whole(block):
-        pltpu.make_async_remote_copy(
-            src_ref=weights.at[block, core], dst_ref=weights.at[block, core],
-            send_sem=w_send.at[block, 0, 0], recv_sem=x_recv.at[block],
-            device_id={"ch": across}, device_id_type=MESH,
-        ).wait_recv()
+    def wait_quarter(block):
+        sum_of(quarter(block, y), w_send.at[0], w_recv.at[block]).wait_recv()
 
     def on_core(which):
         return pl.when(core == which)
@@ -246,11 +234,11 @@
 
     def weights_second():
         for block in column[1:]:
-            wait_quarter(block, y)
+            wait_quarter(block)
 
             @on_core(0)
             def _():
-                steps_of_four(lambda step: along_y(block, step).start())
+                steps_of_four(lambda step: along_y(block, step, True).start())
 
             @on_core(1)
             def _():
@@ -260,66 +248,45 @@
         @on_core(0)
         def _():
             for block in column[1:]:
-                steps_of_four(lambda step: wait_quarter(block, lax.rem(y + step, 4)))
+                three = weights.at[block, core, pl.ds(0, 48)]
+                sum_of(three, w_send.at[0], y_recv.at[block]).wait_recv()
                 steps_of_four(lambda step: along_x(block, step, True).start())
 
         @on_core(1)
         def _():
             for block in column[1:]:
-                steps_of_four(lambda step: along_y(block, step).start())
+                steps_of_four(lambda step: along_y(block, step, False).start())
 
             def onward(block):
-                wait_quarter(block, y)
-                steps_of_four(lambda step: along_y(block, step).start())
+                wait_quarter(block)
+                steps_of_four(lambda step: along_y(block, step, False).start())
 
             other_columns(onward)
 
     def weights_gathered():
         @on_core(0)
         def _():
-            other_columns(wait_whole)
+            sum_of(weights.at[pl.ds(0, 12), core], w_send.at[0], x_recv.at[0]).wait_recv()
 
         @on_core(1)
         def _():
-            @pl.loop(1, CH)
+            @pl.loop(1, 4)
             def _(step):
-                block = lax.rem(h + step, CH)
-                steps_of_four(lambda turn: wait_quarter(block, lax.rem(y + turn, 4)))
+                part = weights.at[pl.ds(0, CH - 1), core, pl.ds(0, 16)]
+                sum_of(part, w_send.at[0], y_recv.at[lax.rem(y + step, 4)]).wait_recv()
 
     def weights_drain():
-        for i in range(3):
-            along_z(i).wait_send()
-
-        @on_core(0)
-        def _():
-            for block in column:
-                steps_of_four(lambda step: along_x(block, step, True).wait_send())
-            for block in column[1:]:
-                steps_of_four(lambda step: along_y(block, step).wait_send())
-
-        @on_core(1)
-        def _():
-            for block in column:
-                steps_of_four(lambda step: along_x(block, step, False).wait_send())
-
-            @pl.loop(1, CH)
-            def _(step):
-                block = lax.rem(h + step, CH)
-                steps_of_four(lambda turn: along_y(block, turn).wait_send())
+        sum_of(weights.at[pl.ds(0, CH - 1), core], w_send.at[0], x_recv.at[0]).wait_send()
 
     def core_copy(block):
         return pltpu.make_async_remote_copy(
             src_ref=weights.at[block, core], dst_ref=weights.at[block, core],
-            send_sem=core_send.at[block], recv_sem=core_recv.at[block],
+            send_sem=core_send.at[0], recv_sem=core_recv.at[0],
             device_id={"ctx": sibling}, device_id_type=MESH,
         )
 
-    def core_arrival(block):
-        return pltpu.make_async_remote_copy(
-            src_ref=weights.at[block, 1 - core], dst_ref=weights.at[block, 1 - core],
-            send_sem=core_send.at[block], recv_sem=core_recv.at[block],
-            device_id={"ctx": sibling}, device_id_type=MESH,
-        )
+    def core_sum():
+        return sum_of(weights.at[pl.ds(0, CH - 1), 1 - core], core_send.at[0], core_recv.at[0])
 
     loads[0].wait()
     for tile in range(TILES):
@@ -376,14 +343,14 @@
         return lambda which: both[:, 8 * which : 8 * which + 8, :].reshape(128, 128)
 
     for g in range(GROUPS):
-        wait_exchange(0, g, f_out, f_in)
+        wait_exchange(0, g, f_in)
         for pair in range(MINE // 2):
             response[g, pair] = spectrum_pair(loader(f_in, g, pair), squares, tw_re, tw_im)
 
 
     weights_second()
     for g in range(GROUPS):
-        wait_exchange(1, g, p_out, p_in)
+        wait_exchange(1, g, p_in)
         for pair in range(MINE // 2):
             signal = spectrum_pair(loader(p_in, g, pair), squares, tw_re, tw_im)
             low, high = inverse_pair(signal, response[g, pair], squares, finals, tw_re, tw_im)
@@ -397,12 +364,12 @@
         peer = 8 * half + tile
         return pltpu.make_async_remote_copy(
             src_ref=hidden.at[g, tile], dst_ref=hidden_in.at[g, h],
-            send_sem=h_send.at[g, peer], recv_sem=h_recv.at[g, h],
+            send_sem=h_send.at[g], recv_sem=h_recv.at[g],
             device_id={"ch": peer}, device_id_type=MESH,
         )
 
     for g in range(GROUPS):
-        wait_exchange(2, g, y_out, y_in)
+        wait_exchange(2, g, y_in)
         for fourth in range(4):
             rows = slice(PART * TILES // 4 * fourth, PART * TILES // 4 * (fourth + 1))
             whole = slice(PART * TILES * g + rows.start, PART * TILES * g + rows.stop)
@@ -430,14 +397,12 @@
     def _(step):
         core_copy(lax.rem(h + step, CH)).start()
 
-    @pl.loop(1, CH)
-    def _(step):
-        core_arrival(lax.rem(h + step, CH)).wait_recv()
+    core_sum().wait_recv()
 
     def mixed_copy(tile):
         return pltpu.make_async_remote_copy(
             src_ref=mixed.at[tile], dst_ref=out_hbm.at[pl.ds(pl.multiple_of(128 * at, 128), 128), :],
-            send_sem=o_send.at[tile], recv_sem=o_recv.at[at],
+            send_sem=o_send.at[0], recv_sem=o_recv.at[0],
             device_id={"ch": 8 * zb + tile}, device_id_type=MESH,
         )
 
@@ -445,28 +410,27 @@
         mixed.at[at], out_hbm.at[pl.ds(pl.multiple_of(128 * at, 128), 128), :], load_sem.at[0]
     )
 
-    for g in range(GROUPS):
-
-        @pl.loop(1, CH)
-        def _(step):
-            peer = lax.rem(h + step, CH)
-            pltpu.make_async_remote_copy(
-                src_ref=hidden_in.at[g, peer], dst_ref=hidden_in.at[g, peer],
-                send_sem=h_send.at[g, peer], recv_sem=h_recv.at[g, peer],
-                device_id={"ch": peer}, device_id_type=MESH,
-            ).wait_recv()
-
-        for i in range(CH // 2):
-            two = hidden_in[g, 2 * i : 2 * i + 2].astype(F32).reshape(128, 128)
-            lhs[:, 128 * i : 128 * i + 128] = two.T.astype(BF16)
+    def hidden_sum(g):
+        return sum_of(hidden_in.at[g, pl.ds(0, CH - 1)], h_send.at[g], h_recv.at[g])
+
+    for g in range(GROUPS):
+        hidden_sum(g).wait_recv()
+        many = 128 // PART
+        for i in range(CH // many):
+            block = hidden_in[g, many * i : many * i + many].astype(F32).reshape(128, 128)
+            lhs[:, 128 * i : 128 * i + 128] = block.T.astype(BF16)
 
         for part in range(4):
             cut = slice(256 * part, 256 * part + 256)
-            value = mul(lhs[...], weights[:, g, :, cut].reshape(CH * PART, 256))
+            side, first = 2 * g // GROUPS, PART * g % 64
+            rhs = weights[:, side, first : first + PART, cut].reshape(CH * PART, 256)
+            value = mul(lhs[...], rhs)
+            if g > 0:
+                value += total[:, cut]
             if g < GROUPS - 1:
                 total[:, cut] = value
                 continue
-            value = (total[:, cut] + value).astype(BF16)
+            value = value.astype(BF16)
             for i in range(2):
                 tile = 2 * part + i
                 mixed[tile] = value[:, 128 * i : 128 * i + 128]
@@ -480,37 +444,14 @@
                     own_copy.start()
 
     for g in range(GROUPS):
-
-        @pl.loop(1, CTX)
-        def _(step):
-            arrival(0, g, f_out, f_in, step).wait_send()
-            arrival(1, g, p_out, p_in, step).wait_send()
-            arrival(2, g, y_out, y_in, step).wait_send()
-
+        for kind, target in enumerate((f_in, p_in, y_in)):
+            pieces(kind, g, target).wait_send()
+        hidden_sum(g).wait_send()
     weights_drain()
-
-    @pl.loop(1, CH)
-    def _(step):
-        core_copy(lax.rem(h + step, CH)).wait_send()
-
-    @pl.loop(0, TILES)
-    def _(step):
-        tile = lax.rem(at + step, TILES)
-        for g in range(GROUPS):
-            hidden_copy(g, 1 - zb, tile).wait_send()
-
-        @pl.when(step > 0)
-        def _():
-            for g in range(GROUPS):
-                hidden_copy(g, zb, tile).wait_send()
-            mixed_copy(tile).wait_send()
-            pltpu.make_async_remote_copy(
-                src_ref=mixed.at[tile],
-                dst_ref=out_hbm.at[pl.ds(pl.multiple_of(128 * tile, 128), 128), :],
-                send_sem=o_send.at[tile], recv_sem=o_recv.at[tile],
-                device_id={"ch": 8 * zb + tile}, device_id_type=MESH,
-            ).wait_recv()
-
+    core_sum().wait_send()
+    seven = sum_of(mixed.at[pl.ds(0, TILES - 1)], o_send.at[0], o_recv.at[0])
+    seven.wait_send()
+    seven.wait_recv()
     own_copy.wait()
 
 
@@ -557,18 +498,18 @@
             pltpu.VMEM((TILES, 128, LANES), BF16),
             dma((11,)),
             dma((2,)),
-            dma((3, GROUPS, CTX)),
-            dma((3, GROUPS, CTX)),
-            dma((3,)),
-            dma((CH, 4, 2)),
-            dma((CH, 4)),
+            dma((3, GROUPS)),
+            dma((3, GROUPS)),
+            dma((1,)),
             dma((CH,)),
             dma((CH,)),
-            dma((CH,)),
-            dma((GROUPS, CH)),
-            dma((GROUPS, CH)),
-            dma((TILES,)),
-            dma((TILES,)),
+            dma((1,)),
+            dma((1,)),
+            dma((1,)),
+            dma((GROUPS,)),
+            dma((GROUPS,)),
+            dma((1,)),
+            dma((1,)),
         ],
         compiler_params=pltpu.CompilerParams(
             collective_id=0, has_side_effects=True, vmem_limit_bytes=60 * 1024 * 1024

time: 63 us -> 58.7 us (0.932)
  Pallas kernels: 61.2 us -> 56.9 us
    pallas_call x1, Pallas kernels: 61.2 us -> 56.9 us  [per_device(): pl.pallas_call(kernel, out_shape=jax.ShapeDtypeStruct((ROWS, LANES), BF16...]
where the time goes in v4:
time: 58.7 us; the launch traced here: 58.6 us
  Pallas kernels  56.9 us (97%)
  local copies, waits for them, and re-layouts  1.67 us (3%)
    pallas_call x1, Pallas kernels, per_device(): pl.pallas_call(kernel, out_shape=jax.ShapeDtypeStruct((ROWS, LANES), BF16...  56.9 us
    unnamed x1, local copies, waits for them, and re-layouts  1.67 us

profile of v4, /device:TPU:1, one launch (start us, length us, event | category | flops | bytes accessed | tf_op | source)
XLA Modules:
  0.0 58.6 jit_solution(4328876335875645837)
XLA Ops:
  0.0 56.9 %shard_map.100 = bf16[1024,128]{1,0:T(8,128)(2,1)} custom-call(bf16[1024,128]{1,0:T(8,128)(2,1)} %q_hbm.1, bf16[1024,128]{1,0:T(8,128)(2,1)} %k_hbm.1, bf16[1024,128]{1,0:T(8,128)(2,1)} %v_hbm.1, f32[3,3,128]{2,1,0:T(4,128)} %taps_hbm.1, f32[1024,128]{1,0:T(8,128)} %filt_hbm.1, f32[1,128]{1,0:T(1,128)} %bitcast.1, bf16[128,2048]{1,0:T(8,128)(2,1)} %w_hbm.1, ...), custom_call_target="tpu_custom_call" | custom-call | flops 3000000000 | bytes 4000000 | tf_op jit(solution)/shard_map/pallas_call | solution.py:463
  56.9 1.7 %copy.12 = bf16[1024,128]{1,0:T(8,128)(2,1)} copy(bf16[1024,128]{1,0:T(8,128)(2,1)} %shard_map.100) | data formatting | bytes 524288

commit v5 on v4

--- a/solution.py
+++ b/solution.py
@@ -60,19 +60,18 @@
     return jnp.dot(a, b, preferred_element_type=F32)
 
 
-def spectrum_pair(load, squares, tw_re, tw_im):
-    points = jnp.concatenate([load(0), load(1)], axis=1).astype(BF16)
+def spectrum(channels, squares, tw_re, tw_im):
+    points = jnp.concatenate(channels, axis=1).astype(BF16)
     stage = mul(squares[0], jnp.concatenate([points, points], axis=0))
     parts = []
-    for which in range(2):
-        re = stage[:128, 128 * which : 128 * which + 128]
-        im = stage[128:, 128 * which : 128 * which + 128]
+    for i in range(len(channels)):
+        re, im = stage[:128, 128 * i : 128 * i + 128], stage[128:, 128 * i : 128 * i + 128]
         parts.append(jnp.concatenate([re * tw_re - im * tw_im, re * tw_im + im * tw_re], axis=1))
     high, low = split(jnp.concatenate(parts, axis=0))
     return mul(high, squares[1]) + mul(low, squares[1]) + mul(high, squares[2])
 
 
-def inverse_pair(signal, response, squares, finals, tw_re, tw_im):
+def causal(signal, response, squares, finals, tw_re, tw_im):
     s_re, s_im = signal[:, :128], signal[:, 128:]
     r_re, r_im = response[:, :128], response[:, 128:]
     high, low = split(
@@ -80,13 +79,11 @@
     )
     stage = mul(high, squares[3]) + mul(low, squares[3]) + mul(high, squares[4])
     turned = []
-    for which in range(2):
-        re = stage[128 * which : 128 * which + 128, :128]
-        im = stage[128 * which : 128 * which + 128, 128:]
+    for i in range(signal.shape[0] // 128):
+        re, im = stage[128 * i : 128 * i + 128, :128], stage[128 * i : 128 * i + 128, 128:]
         turned.append(jnp.concatenate([re * tw_re + im * tw_im, im * tw_re - re * tw_im], axis=0))
     high, low = split(jnp.concatenate(turned, axis=1))
-    both = mul(finals[0], high) + mul(finals[0], low) + mul(finals[1], high)
-    return both[:, :128], both[:, 128:]
+    return mul(finals[0], high) + mul(finals[0], low) + mul(finals[1], high)
 
 
 def kernel(
@@ -120,8 +117,7 @@
             ]
         )
     ]
-    for load in loads:
-        load.start()
+    loads[0].start()
 
     barrier = pltpu.get_barrier_semaphore()
 
@@ -130,9 +126,15 @@
         pl.semaphore_signal(
             barrier, inc=1, device_id={"ctx": lax.rem(c + step, CTX)}, device_id_type=MESH
         )
+
+    @pl.loop(1, 16)
+    def _(step):
         pl.semaphore_signal(
             barrier, inc=1, device_id={"ch": lax.rem(h + step, CH)}, device_id_type=MESH
         )
+
+    for load in loads[1:]:
+        load.start()
 
     def turn(target, tile, value):
         target[pl.ds(tile, LANES, stride=TILES), :] = value.T
@@ -338,25 +340,21 @@
 
     tw_re, tw_im = twiddle[0], twiddle[1]
 
-    def loader(source, g, pair):
-        both = source[g, :, 16 * pair : 16 * pair + 16, :].astype(F32)
-        return lambda which: both[:, 8 * which : 8 * which + 8, :].reshape(128, 128)
+    def channels(source, g):
+        parts = source[g].astype(F32)
+        return [parts[:, 8 * i : 8 * i + 8, :].reshape(128, 128) for i in range(MINE)]
 
     for g in range(GROUPS):
         wait_exchange(0, g, f_in)
-        for pair in range(MINE // 2):
-            response[g, pair] = spectrum_pair(loader(f_in, g, pair), squares, tw_re, tw_im)
-
+        response[g] = spectrum(channels(f_in, g), squares, tw_re, tw_im)
 
     weights_second()
     for g in range(GROUPS):
         wait_exchange(1, g, p_in)
-        for pair in range(MINE // 2):
-            signal = spectrum_pair(loader(p_in, g, pair), squares, tw_re, tw_im)
-            low, high = inverse_pair(signal, response[g, pair], squares, finals, tw_re, tw_im)
-            y_out[g, :, 16 * pair : 16 * pair + 16, :] = jnp.concatenate(
-                [low.reshape(CTX, TILES, 128), high.reshape(CTX, TILES, 128)], axis=1
-            ).astype(BF16)
+        signal = spectrum(channels(p_in, g), squares, tw_re, tw_im)
+        conv = causal(signal, response[g], squares, finals, tw_re, tw_im)
+        rows = [conv[:, 128 * i : 128 * i + 128].reshape(CTX, TILES, 128) for i in range(MINE)]
+        y_out[g] = jnp.concatenate(rows, axis=1).astype(BF16)
         start_exchange(2, g, y_out, y_in)
 
     weights_third()
@@ -488,7 +486,7 @@
             pltpu.VMEM(piece, BF16),
             pltpu.VMEM(piece, BF16),
             pltpu.VMEM(piece, BF16),
-            pltpu.VMEM((GROUPS, MINE // 2, 256, 256), F32),
+            pltpu.VMEM((GROUPS, MINE * 128, 256), F32),
             pltpu.VMEM((PART * TILES, 128), F32),
             pltpu.VMEM((GROUPS, TILES, PART, 128), BF16),
             pltpu.VMEM((GROUPS, CH, PART, 128), BF16),

time: 58.7 us -> 57.5 us (0.980)
  Pallas kernels: 56.9 us -> 55.4 us
    pallas_call x1, Pallas kernels: 56.9 us -> 55.4 us  [per_device(): pl.pallas_call(kernel, out_shape=jax.ShapeDtypeStruct((ROWS, LANES), BF16...]
where the time goes in v5:
time: 57.5 us; the launch traced here: 57.1 us
  Pallas kernels  55.4 us (96%)
  local copies, waits for them, and re-layouts  1.67 us (3%)
    pallas_call x1, Pallas kernels, per_device(): pl.pallas_call(kernel, out_shape=jax.ShapeDtypeStruct((ROWS, LANES), BF16...  55.4 us
    unnamed x1, local copies, waits for them, and re-layouts  1.67 us

profile of v5, /device:TPU:1, one launch (start us, length us, event | category | flops | bytes accessed | tf_op | source)
XLA Modules:
  0.0 57.1 jit_solution(17079043709665985889)
XLA Ops:
  0.0 55.4 %shard_map.100 = bf16[1024,128]{1,0:T(8,128)(2,1)} custom-call(bf16[1024,128]{1,0:T(8,128)(2,1)} %q_hbm.1, bf16[1024,128]{1,0:T(8,128)(2,1)} %k_hbm.1, bf16[1024,128]{1,0:T(8,128)(2,1)} %v_hbm.1, f32[3,3,128]{2,1,0:T(4,128)} %taps_hbm.1, f32[1024,128]{1,0:T(8,128)} %filt_hbm.1, f32[1,128]{1,0:T(1,128)} %bitcast.1, bf16[128,2048]{1,0:T(8,128)(2,1)} %w_hbm.1, ...), custom_call_target="tpu_custom_call" | custom-call | flops 3000000000 | bytes 4000000 | tf_op jit(solution)/shard_map/pallas_call | solution.py:461
  55.4 1.7 %copy.12 = bf16[1024,128]{1,0:T(8,128)(2,1)} copy(bf16[1024,128]{1,0:T(8,128)(2,1)} %shard_map.100) | data formatting | bytes 524288

commit v6 on v5

--- a/solution.py
+++ b/solution.py
@@ -299,7 +299,6 @@
         load.wait()
     for i, source in enumerate((k_in, v_in, q_in)):
         halo_out[16 * i : 16 * i + 16, :] = source[ROWS - 16 :, :]
-        ext[i, 8:, :] = source[...].astype(F32)
 
     def smooth(tile):
         first = 128 * tile + 8
@@ -314,9 +313,6 @@
         turn(skipped_t, tile, skip[...] * both)
         turn(gate_t, tile, sums[2])
 
-    for tile in range(1, TILES):
-        smooth(tile)
-
     pl.semaphore_wait(barrier, 30)
 
     halo = pltpu.make_async_remote_copy(
@@ -327,6 +323,11 @@
     for g in range(GROUPS):
         start_exchange(0, g, f_out, f_in)
     weights_start()
+
+    for i, source in enumerate((k_in, v_in, q_in)):
+        ext[i, 8:, :] = source[...].astype(F32)
+    for tile in range(1, TILES):
+        smooth(tile)
 
     halo.wait()
     for i in range(3):

time: 57.5 us -> 57.4 us (level)
  no operation moved by 1% of the time
where the time goes in v6:
time: 57.4 us; the launch traced here: 56.9 us
  Pallas kernels  55.2 us (96%)
  local copies, waits for them, and re-layouts  1.67 us (3%)
    pallas_call x1, Pallas kernels, per_device(): pl.pallas_call(kernel, out_shape=jax.ShapeDtypeStruct((ROWS, LANES), BF16...  55.2 us
    unnamed x1, local copies, waits for them, and re-layouts  1.67 us

profile of v6, /device:TPU:1, one launch (start us, length us, event | category | flops | bytes accessed | tf_op | source)
XLA Modules:
  0.0 56.9 jit_solution(17542028977021195661)
XLA Ops:
  0.0 55.2 %shard_map.100 = bf16[1024,128]{1,0:T(8,128)(2,1)} custom-call(bf16[1024,128]{1,0:T(8,128)(2,1)} %q_hbm.1, bf16[1024,128]{1,0:T(8,128)(2,1)} %k_hbm.1, bf16[1024,128]{1,0:T(8,128)(2,1)} %v_hbm.1, f32[3,3,128]{2,1,0:T(4,128)} %taps_hbm.1, f32[1024,128]{1,0:T(8,128)} %filt_hbm.1, f32[1,128]{1,0:T(1,128)} %bitcast.1, bf16[128,2048]{1,0:T(8,128)(2,1)} %w_hbm.1, ...), custom_call_target="tpu_custom_call" | custom-call | flops 3000000000 | bytes 4000000 | tf_op jit(solution)/shard_map/pallas_call | solution.py:462
  55.2 1.7 %copy.12 = bf16[1024,128]{1,0:T(8,128)(2,1)} copy(bf16[1024,128]{1,0:T(8,128)(2,1)} %shard_map.100) | data formatting | bytes 524288
